TPU v7x, 256 devices: a whole 4x4x8 slice. The times are simulated.
256 devices in a mesh: group: 16 (over z, core), tp: 16 (over y, x).
Axes of the slice: x: 4, y: 4, z: 8, core: 2. Of those that a mesh axis runs over, the one named last changes fastest.
Arguments:
- prompt_states: bfloat16 [64, 64, 4096], P('group', None, 'tp')
- ctx_weight: bfloat16 [4096, 3072], P('tp'), may hold values from -0.125 to 0.125
- image_prompt: int32 [64], replicated, may hold values from 0 to 63, each once
- image_lengths: int32 [16, 4], P('group'), may hold values from 1 to 128, 256 in all within a row
- latents: bfloat16 [16, 256, 3072], P('group', 'tp'), may hold values from -6 to 6
- img_mod: float32 [16, 4, 2, 3, 3072], P('group'), may hold values from -3 to 3
- txt_mod: float32 [16, 4, 2, 2, 3072], P('group'), may hold values from -3 to 3
- img_qkv: bfloat16 [3072, 3, 2048], P(None, None, 'tp'), may hold values from -0.109375 to 0.109375
- txt_kv: bfloat16 [3072, 2, 2048], P(None, None, 'tp'), may hold values from -0.109375 to 0.109375
- qk_gain: float32 [3, 128], replicated, may hold values from 0.7 to 2.2
- img_proj: bfloat16 [2048, 3072], P('tp'), may hold values from -0.125 to 0.125
Outputs:
- denoised: bfloat16 [16, 256, 3072], P('group', 'tp')
Inputs may be any that keep to these rules, and one draw needn't show every extreme that they name: `image_prompt`: image 4 * g + k is image k of group g; every prompt conditions exactly one image. `image_lengths`: the image tokens of a group sum to 256; every group has one image of exactly 128 tokens.
All inputs are finite; a program needn't handle non-finite values.
Results may differ from a plain program's by a relative error of at most 0.025.
Values may be sent and summed in bfloat16 or wider, within the bound.
A program may use at most 64 MiB of HBM per device.

v0:
```python
import jax
import jax.numpy as jnp
from jax import lax
from jax.sharding import PartitionSpec as P


def rms_scale(values, gain_row):
    return values * lax.rsqrt(jnp.mean(values * values, -1, keepdims=True) + 1e-06) * gain_row


def attend_block(query_block, segment_block, keys_all, values_all, segment_keys, head_dim):
    scores = jnp.einsum(
        "qhd,khd->hqk", query_block, keys_all, preferred_element_type=jnp.float32
    ) * head_dim ** (-0.5)
    allowed = (segment_block[:, None] == segment_keys[None, :])[None]
    expsum = jnp.where(allowed, jnp.exp(scores), 0.0)
    weights = (expsum / jnp.sum(expsum, -1, keepdims=True)).astype(jnp.bfloat16)
    return jnp.einsum(
        "hqk,khd->qhd", weights, values_all, preferred_element_type=jnp.float32
    ).astype(jnp.bfloat16)


def attention(queries, keys_all, values_all, segment_rows, segment_keys):
    rows_total = queries.shape[0]
    head_dim = queries.shape[2]
    block_rows = min(512, rows_total)
    block_count = rows_total // block_rows
    query_blocks = queries.reshape((block_count, block_rows) + queries.shape[1:])
    segment_blocks = segment_rows.reshape(block_count, block_rows)

    def attend_pair(packed):
        return attend_block(packed[0], packed[1], keys_all, values_all, segment_keys, head_dim)

    outputs = lax.map(attend_pair, (query_blocks, segment_blocks))
    return outputs.reshape(rows_total, -1)


def on_device(
    prompt_states,
    ctx_weight,
    image_prompt,
    image_lengths,
    latents,
    img_mod,
    txt_mod,
    img_qkv,
    txt_kv,
    qk_gain,
    img_proj,
):
    per_rank, text_tokens, width_local = prompt_states.shape
    text_rows = per_rank * text_tokens
    tp_count = lax.axis_size("tp")
    model_width = ctx_weight.shape[1]
    width_slice = model_width // tp_count
    head_dim = qk_gain.shape[1]
    heads_local = img_qkv.shape[2] // head_dim
    rows_local = latents.shape[1]
    image_rows = rows_local * tp_count
    step_count = img_mod.shape[2]
    group_index = lax.axis_index("group")
    tp_index = lax.axis_index("tp")
    text_local = prompt_states.reshape(text_rows, width_local)
    embedded = lax.psum_scatter(
        lax.dot_general(
            ctx_weight, text_local, (((0,), (1,)), ((), ())), preferred_element_type=jnp.float32
        ).astype(jnp.bfloat16),
        "tp",
        scatter_dimension=0,
        tiled=True,
    )
    embedded = embedded.reshape(width_slice, per_rank, text_tokens)
    wanted = lax.dynamic_slice_in_dim(image_prompt, group_index * per_rank, per_rank)
    every_prompt = lax.all_gather(embedded, "group", axis=1, tiled=True)
    slot_text = jnp.take(every_prompt, wanted, axis=1)
    slot_flat = slot_text.reshape(width_slice, text_rows)
    text_full = lax.all_gather(slot_flat, "tp", axis=0, tiled=True).astype(jnp.float32)
    text_center = text_full - jnp.mean(text_full, 0, keepdims=True)
    text_normed = text_center * lax.rsqrt(
        jnp.mean(text_center * text_center, 0, keepdims=True) + 1e-06
    )
    text_normed = text_normed.reshape(model_width, per_rank, text_tokens)
    text_segments = jnp.repeat(jnp.arange(per_rank, dtype=jnp.int32), text_tokens)
    bounds = jnp.cumsum(image_lengths[0])
    row_ids = jnp.arange(image_rows, dtype=jnp.int32)
    segment_all = jnp.sum((row_ids[:, None] >= bounds[None, :]).astype(jnp.int32), 1)
    segment_keys = jnp.concatenate([text_segments, segment_all])
    onehot_all = (segment_all[:, None] == jnp.arange(per_rank, dtype=jnp.int32)[None, :]).astype(
        jnp.float32
    )
    onehot_mine = lax.dynamic_slice_in_dim(onehot_all, tp_index * rows_local, rows_local, 0)
    image_mod = img_mod[0]
    text_mod = txt_mod[0]

    def per_row(onehot, mod_table):
        return jnp.dot(onehot, mod_table, precision=lax.Precision.HIGHEST)

    latent_mine = latents[0]
    for step_index in range(step_count):
        values = latent_mine.astype(jnp.float32)
        centered = values - jnp.mean(values, -1, keepdims=True)
        normed = centered * lax.rsqrt(jnp.mean(centered * centered, -1, keepdims=True) + 1e-06)
        shift_rows = per_row(onehot_mine, image_mod[:, step_index, 0])
        scale_img = per_row(onehot_mine, image_mod[:, step_index, 1])
        modulated = (normed * (1.0 + scale_img) + shift_rows).astype(jnp.bfloat16)
        piece_rows = lax.all_gather(modulated, "tp", axis=0, tiled=True)
        projected = lax.dot_general(
            piece_rows, img_qkv, (((1,), (0,)), ((), ())), preferred_element_type=jnp.float32
        )
        projected = projected.reshape(piece_rows.shape[0], 3, heads_local, head_dim)
        queries = rms_scale(projected[:, 0], qk_gain[0])
        keys_img = rms_scale(projected[:, 1], qk_gain[1])
        stacked = jnp.stack([queries, keys_img, projected[:, 2]], 1).astype(jnp.bfloat16)
        text_scale = jnp.transpose(text_mod[:, step_index, 1])[:, :, None]
        text_shift = jnp.transpose(text_mod[:, step_index, 0])[:, :, None]
        text_in = (
            (text_normed * (1.0 + text_scale) + text_shift)
            .astype(jnp.bfloat16)
            .reshape(model_width, text_rows)
        )
        text_kv = lax.dot_general(
            text_in, txt_kv, (((0,), (0,)), ((), ())), preferred_element_type=jnp.float32
        )
        text_kv = text_kv.reshape(text_rows, 2, heads_local, head_dim)
        keys_text = rms_scale(text_kv[:, 0], qk_gain[2]).astype(jnp.bfloat16)
        vals_text = text_kv[:, 1].astype(jnp.bfloat16)
        keys_all = jnp.concatenate([keys_text, stacked[:, 1]], 0)
        values_all = jnp.concatenate([vals_text, stacked[:, 2]], 0)
        attended = attention(stacked[:, 0], keys_all, values_all, segment_all, segment_keys)
        update = lax.psum_scatter(
            jnp.dot(attended, img_proj, preferred_element_type=jnp.float32).astype(jnp.bfloat16),
            "tp",
            scatter_dimension=0,
            tiled=True,
        ).astype(jnp.float32)
        gate_rows = per_row(onehot_mine, image_mod[:, step_index, 2])
        latent_mine = (latent_mine.astype(jnp.float32) + gate_rows * update).astype(jnp.bfloat16)
    return latent_mine[None]


def solution(mesh):
    placed = (
        P("group", None, "tp"),
        P("tp", None),
        P(),
        P("group", None),
        P("group", "tp", None),
        P("group", None, None, None, None),
        P("group", None, None, None, None),
        P(None, None, "tp"),
        P(None, None, "tp"),
        P(),
        P("tp", None),
    )
    return jax.shard_map(
        on_device, mesh=mesh, in_specs=placed, out_specs=P("group", "tp", None), check_vma=False
    )
```

profile of v0, /device:TPU:32, one launch (start us, length us, event | category | flops | bytes accessed | tf_op | source)
XLA Modules:
  0.0 472.6 jit_solution(12731927197142993557)
XLA Ops:
  6.5 3.4 convolution_convert_fusion.2
  9.9 0.0 reduce-scatter.4.cloned.1.call-update
  10.0 0.0 all-gather.5.cloned.1.call-start
  10.0 82.1 %reduce-scatter.4.cloned.1.call-done = bf16[192,256]{1,0:T(8,128)(2,1)} async-done(((bf16[3072,256]{1,0:T(8,128)(2,1)}), bf16[192,256]{1,0:T(8,128)(2,1)}) %reduce-scatter.4.cloned.1.call-update) | async-done | bytes 98320 | tf_op jit(solution)/shard_map/reduce_scatter | solution.py:64
  92.1 1.7 copy.37
  93.8 0.0 all-gather.5.cloned.1.call-update
  93.8 0.0 all-gather.9.cloned.1.call-start
  93.9 0.2 reduce-window.8
  94.0 0.1 convert_reduce_fusion.2
  94.1 0.1 dynamic-slice.1
  94.2 0.1 convert_reduce_fusion.1
  94.4 0.2 fusion.53
  94.6 0.8 fusion.104
  95.4 0.3 fusion.6
  95.7 0.9 fusion.10
  96.7 0.0 all-gather.9.cloned.1.call-update
  96.7 0.0 all-gather.7.cloned.1.call-start
  96.8 0.1 compare_and_fusion
  96.8 0.1 broadcast_in_dim.70
  96.9 0.1 broadcast_in_dim.71
  97.0 0.1 reshape.625
  97.1 0.6 pad_add_fusion
  97.7 0.6 slice_bitcast_fusion.4
  98.3 34.1 %all-gather.5.cloned.1.call-done = bf16[192,64,64]{0,2,1:T(8,128)(2,1)} async-done(((bf16[192,4,64]{0,2,1:T(8,128)(2,1)}), bf16[192,64,64]{0,2,1:T(8,128)(2,1)}) %all-gather.5.cloned.1.call-update) | async-done | bytes 1572880 | tf_op jit(solution)/shard_map/all_gather | solution.py:74
  132.3 2.1 gather_fusion
  134.5 0.1 copy.38
  134.6 0.6 broadcast_select_fusion
  135.3 0.0 reduce-scatter.6.cloned.1.call-start
  135.3 0.2 slice_add_fusion
  135.6 47.2 %all-gather.9.cloned.1.call-done = bf16[256,3072]{1,0:T(8,128)(2,1)} async-done(((bf16[16,3072]{1,0:T(8,128)(2,1)}), bf16[256,3072]{1,0:T(8,128)(2,1)}) %all-gather.9.cloned.1.call-update) | async-done | bytes 1572880 | tf_op jit(solution)/shard_map/all_gather | solution.py:106
  182.8 2.4 fusion.33
  185.2 0.1 multiply_reduce_fusion.6
  185.3 0.6 add_rsqrt_fusion.3
  186.0 0.1 fusion.68
  186.1 47.4 %all-gather.7.cloned.1.call-done = bf16[3072,256]{1,0:T(8,128)(2,1)} async-done(((bf16[192,256]{1,0:T(8,128)(2,1)}), bf16[3072,256]{1,0:T(8,128)(2,1)}) %all-gather.7.cloned.1.call-update) | async-done | bytes 1572880 | tf_op jit(solution)/shard_map/all_gather | solution.py:77
  233.5 2.6 copy.39
  236.1 1.8 convert_reduce_fusion
  237.9 0.1 copy-done.1
  238.0 0.6 fusion.18
  238.5 1.1 fusion.17
  239.7 0.3 copy-done.24
  239.9 0.6 fusion.39
  240.5 0.1 multiply_reduce_fusion.2
  240.7 0.6 fusion.25
  241.3 0.1 multiply_reduce_fusion.5
  241.5 0.8 multiply_convert_fusion.1
  242.2 2.0 fusion.105
  244.2 3.2 convolution_convert_fusion.1
  247.5 0.0 all-gather.11.cloned.1.call-start
  247.5 78.2 %reduce-scatter.6.cloned.1.call-done = bf16[16,3072]{1,0:T(8,128)(2,1)} async-done(((bf16[256,3072]{1,0:T(8,128)(2,1)}), bf16[16,3072]{1,0:T(8,128)(2,1)}) %reduce-scatter.6.cloned.1.call-update) | async-done | bytes 98320 | tf_op jit(solution)/shard_map/reduce_scatter | solution.py:130
  325.7 1.3 fusion.106
  327.0 0.2 multiply_reduce_fusion
  327.3 1.1 fusion.4
  328.4 1.7 fusion.12
  330.1 0.0 reduce-scatter.8.cloned.1.call-start
  330.2 0.9 fusion.74
  331.1 47.5 %all-gather.11.cloned.1.call-done = bf16[256,3072]{1,0:T(8,128)(2,1)} async-done(((bf16[16,3072]{1,0:T(8,128)(2,1)}), bf16[256,3072]{1,0:T(8,128)(2,1)}) %all-gather.11.cloned.1.call-update) | async-done | bytes 1572880 | tf_op jit(solution)/shard_map/all_gather | solution.py:106
  378.6 2.4 fusion.36
  381.0 0.1 multiply_reduce_fusion.3
  381.2 0.1 fusion.71
  381.4 1.1 fusion.107
  382.5 3.2 convolution_convert_fusion
  385.7 78.2 %reduce-scatter.8.cloned.1.call-done = bf16[16,3072]{1,0:T(8,128)(2,1)} async-done(((bf16[256,3072]{1,0:T(8,128)(2,1)}), bf16[16,3072]{1,0:T(8,128)(2,1)}) %reduce-scatter.8.cloned.1.call-update) | async-done | bytes 98320 | tf_op jit(solution)/shard_map/reduce_scatter | solution.py:130
  464.0 1.8 fusion.13
  (72 shorter events, 0.3 us)
Async XLA Ops:
  6.5 176.3 %copy-start = (bf16[3072,3,128]{2,0,1:T(8,128)(2,1)S(1)}, bf16[3072,3,128]{2,0,1:T(8,128)(2,1)}, u32[]{:S(2)}) copy-start(bf16[3072,3,128]{2,0,1:T(8,128)(2,1)} %param.18) | copy-start | bytes 7077892
  6.5 85.6 %reduce-scatter.4.cloned.1.call-start = ((), (), s32[]{:S(2)}) async-start(), calls=%async_computation.3 | async-start | bytes 1671168 | tf_op jit(solution)/shard_map/reduce_scatter | solution.py:64
  9.9 84.0 %copy-start.25 = (s32[1,4]{1,0:T(1,128)S(1)}, s32[1,4]{1,0:T(1,128)}, u32[]{:S(2)}) copy-start(s32[1,4]{1,0:T(1,128)} %param.14) | copy-start | bytes 52
  9.9 84.3 %copy-start.3 = (bf16[1,16,3072]{2,1,0:T(8,128)(2,1)S(1)}, bf16[1,16,3072]{2,1,0:T(8,128)(2,1)}, u32[]{:S(2)}) copy-start(bf16[1,16,3072]{2,1,0:T(8,128)(2,1)} %param.15) | copy-start | bytes 294916
  9.9 84.7 %copy-start.6 = (f32[1,4,2,3,3072]{4,2,3,1,0:T(2,128)S(1)}, f32[1,4,2,3,3072]{4,2,3,1,0:T(2,128)}, u32[]{:S(2)}) copy-start(f32[1,4,2,3,3072]{4,2,3,1,0:T(2,128)} %param.16) | copy-start | bytes 884740
  9.9 86.8 %copy-start.21 = (s32[64]{0:T(128)S(1)}, s32[64]{0:T(128)}, u32[]{:S(2)}) copy-start(s32[64]{0:T(128)} %param.13) | copy-start | bytes 772
  9.9 87.8 %copy-start.16 = (f32[3,128]{1,0:T(4,128)S(1)}, f32[3,128]{1,0:T(4,128)}, u32[]{:S(2)}) copy-start(f32[3,128]{1,0:T(4,128)} %param.20) | copy-start | bytes 4612
  9.9 125.4 %copy-start.7 = (f32[1,4,2,2,3072]{4,3,2,1,0:T(2,128)S(1)}, f32[1,4,2,2,3072]{4,3,2,1,0:T(2,128)}, u32[]{:S(2)}) copy-start(f32[1,4,2,2,3072]{4,3,2,1,0:T(2,128)} %param.17) | copy-start | bytes 589828
  10.0 122.4 %all-gather.5.cloned.1.call-start = ((), (), s32[]{:S(2)}) async-start(), calls=%async_computation.4 | async-start | bytes 2228224 | tf_op jit(solution)/shard_map/all_gather | solution.py:74
  93.8 89.0 %all-gather.9.cloned.1.call-start = ((), (), s32[]{:S(2)}) async-start(), calls=%async_computation.6 | async-start | bytes 1671168 | tf_op jit(solution)/shard_map/all_gather | solution.py:106
  94.1 41.4 %copy-start.17 = (s32[256]{0:T(256)}, s32[256]{0:T(256)S(1)}, u32[]{:S(2)}) copy-start(s32[256]{0:T(256)S(1)} %convert_reduce_fusion.2) | copy-start | bytes 3076
  94.2 234.1 %copy-start.9 = (s32[16]{0:T(128)}, s32[16]{0:T(128)S(1)}, u32[]{:S(2)}) copy-start(s32[16]{0:T(128)S(1)} %dynamic-slice.1) | copy-start | bytes 196
  96.7 136.8 %all-gather.7.cloned.1.call-start = ((), (), s32[]{:S(2)}) async-start(), calls=%async_computation.5 | async-start | bytes 1671168 | tf_op jit(solution)/shard_map/all_gather | solution.py:77
  98.3 87.7 %copy-start.11 = (f32[128]{0:T(128)}, f32[128]{0:T(128)S(1)}, u32[]{:S(2)}) copy-start(f32[128]{0:T(128)S(1)} %get-tuple-element.66) | copy-start | bytes 1540
  135.3 190.4 %reduce-scatter.6.cloned.1.call-start = ((), (), s32[]{:S(2)}) async-start(), calls=%async_computation.7 | async-start | bytes 1671168 | tf_op jit(solution)/shard_map/reduce_scatter | solution.py:130
  185.2 0.8 copy-start.4
  236.1 1.9 copy-start.1
  238.5 1.4 copy-start.24
  240.5 0.9 copy-start.5
  240.7 0.8 copy-start.13
  240.7 1.6 copy-start.14
  240.7 1.5 copy-start.18
  240.7 1.5 copy-start.20
  240.7 1.5 copy-start.22
  241.3 2.9 copy-start.2
  247.5 131.1 %all-gather.11.cloned.1.call-start = ((), (), s32[]{:S(2)}) async-start(), calls=%async_computation.8 | async-start | bytes 1671168 | tf_op jit(solution)/shard_map/all_gather | solution.py:106
  330.1 133.8 %reduce-scatter.8.cloned.1.call-start = ((), (), s32[]{:S(2)}) async-start(), calls=%async_computation.9 | async-start | bytes 1671168 | tf_op jit(solution)/shard_map/reduce_scatter | solution.py:130
  331.1 50.1 %copy-start.12 = (f32[128]{0:T(128)S(1)}, f32[128]{0:T(128)}, u32[]{:S(2)}) copy-start(f32[128]{0:T(128)} %copy-done.11) | copy-start | bytes 1540
  331.1 50.3 %copy-start.15 = (s32[512]{0:T(512)S(1)}, s32[512]{0:T(512)}, u32[]{:S(2)}) copy-start(s32[512]{0:T(512)} %pad_add_fusion) | copy-start | bytes 6148
  331.1 50.3 %copy-start.19 = (s32[256]{0:T(256)S(1)}, s32[256]{0:T(256)}, u32[]{:S(2)}) copy-start(s32[256]{0:T(256)} %copy-done.17) | copy-start | bytes 3076
  331.1 50.3 %copy-start.23 = (f32[128]{0:T(128)S(1)}, f32[128]{0:T(128)}, u32[]{:S(2)}) copy-start(f32[128]{0:T(128)} %get-tuple-element.65) | copy-start | bytes 1540
  378.6 2.8 copy-start.8
  382.5 81.5 %copy-start.10 = (s32[16]{0:T(128)S(1)}, s32[16]{0:T(128)}, u32[]{:S(2)}) copy-start(s32[16]{0:T(128)} %copy-done.9) | copy-start | bytes 196
Sparse Core Ops, SparseCore 0:
  10.9 81.2 reduce-scatter.3
  94.0 38.3 all-gather.4
  134.8 47.9 all-gather.8
  185.1 48.3 all-gather.6
  247.6 78.0 reduce-scatter.5
  330.2 48.3 all-gather.10
  385.8 78.0 reduce-scatter.7
where the time goes:
time: 473 us
  waiting for transfers between devices  415 us (88%)
  matrix products  26 us (5%)
  between operations  13.9 us (3%)
  local copies, waits for them, and re-layouts  9.65 us (2%)
  other arithmetic  7.93 us (2%)
    reduce_scatter x2, waiting for transfers between devices, on_device(): lax.psum_scatter(jnp.dot(attended, img_proj, preferred_element_type=jnp.f...  156 us
    all_gather x2, waiting for transfers between devices, on_device(): piece_rows = lax.all_gather(modulated, 'tp', axis=0, tiled=True)  94.7 us
    reduce_scatter x1, waiting for transfers between devices, on_device(): lax.psum_scatter(lax.dot_general(ctx_weight, text_local, (((0,), (1,)), (...  82.1 us
    all_gather x1, waiting for transfers between devices, on_device(): lax.all_gather(slot_flat, 'tp', axis=0, tiled=True).astype(jnp.float32)  47.4 us
    all_gather x1, waiting for transfers between devices, on_device(): every_prompt = lax.all_gather(embedded, 'group', axis=1, tiled=True)  34.1 us
  transfers between devices with their start and end apart: 7, of which 7 were waited for; matrix products, arithmetic and copies ran while one was open for 2% of the time, Pallas kernels for 0%

commit v1 on v0

v1 whole, which is shorter than its diff:
```python
import functools

import jax
import jax.numpy as jnp
from jax import lax
from jax.experimental import pallas as pl
from jax.experimental.pallas import tpu as pltpu
from jax.sharding import PartitionSpec as P

MESH = pl.DeviceIdType.MESH
F32, BF16 = jnp.float32, jnp.bfloat16
WIDTH, HALF, QUARTER = 3072, 1536, 768
ROWS = 16
SIDE = 4
DEPTH = 8
HEAD = 128
OFFSETS = (0, 3, 1, 2)
RELAY_RIGHT, RELAY_LEFT = (0, 3), (1, 2)


def layer_norm(values):
    centered = values - jnp.mean(values, -1, keepdims=True)
    return centered * lax.rsqrt(jnp.mean(centered * centered, -1, keepdims=True) + 1e-6)


def rms_scale(values, gain_row):
    return values * lax.rsqrt(jnp.mean(values * values, -1, keepdims=True) + 1e-6) * gain_row


class Place:
    def __init__(self):
        self.group, self.tp = lax.axis_index("group"), lax.axis_index("tp")
        self.x, self.y = lax.rem(self.tp, SIDE), self.tp // SIDE
        self.z, self.core = self.group // 2, lax.rem(self.group, 2)

    def along(self, axis, step):
        if axis == 0:
            return (self.group, self.y * SIDE + lax.rem(self.x + step + SIDE, SIDE))
        return (self.group, lax.rem(self.y + step + SIDE, SIDE) * SIDE + self.x)

    def slot(self, half, first, second):
        dx, dy = (first, second) if half == 0 else (second, first)
        return lax.rem(self.y + dy + SIDE, SIDE) * SIDE + lax.rem(self.x + dx + SIDE, SIDE)

    def up(self, step):
        return (lax.rem(self.z + step + DEPTH, DEPTH) * 2 + self.core, self.tp)

    def sibling(self):
        return (self.z * 2 + 1 - self.core, self.tp)


class Sends:
    def __init__(self, sems):
        self.sems, self.pending = sems, []

    def start(self, src, dst, recv, device):
        copy = pltpu.make_async_remote_copy(
            src_ref=src,
            dst_ref=dst,
            send_sem=self.sems.at[len(self.pending)],
            recv_sem=recv,
            device_id=device,
            device_id_type=MESH,
        )
        copy.start()
        self.pending.append(copy)

    def finish(self):
        for copy in self.pending:
            copy.wait_send()


def arrived(ref, sem):
    pltpu.make_async_copy(ref, ref, sem).wait()


class Gather:
    def __init__(self, place, buf, sems, send_sems):
        self.place, self.buf, self.sems, self.sends = place, buf, sems, Sends(send_sems)

    def send(self, half, axis, step, slot, part=None):
        if part is None:
            ref, sem = self.buf.at[half, slot], self.sems.at[half, slot, 0]
        else:
            ref = self.buf.at[half, slot, :, pl.ds(part * QUARTER, QUARTER)]
            sem = self.sems.at[half, slot, part]
        self.sends.start(ref, ref, sem, self.place.along(axis, step))

    def wait(self, half, slot, part=None):
        if part is None:
            ref, sem = self.buf.at[half, slot], self.sems.at[half, slot, 0]
        else:
            ref = self.buf.at[half, slot, :, pl.ds(part * QUARTER, QUARTER)]
            sem = self.sems.at[half, slot, part]
        arrived(ref, sem)

    def start(self):
        place = self.place
        for half in (0, 1):
            first, second = half, 1 - half
            own = place.slot(half, 0, 0)
            for step in (1, -1):
                self.send(half, first, step, own)
            for step in (1, -1):
                self.send(half, second, step, own)

    def neighbours(self):
        place = self.place
        for half in (0, 1):
            first, second = half, 1 - half
            for offset, way, part in ((-1, 1, 0), (1, -1, 1)):
                slot = place.slot(half, offset, 0)
                self.wait(half, slot)
                self.send(half, first, way, slot, part)
                for step in (1, -1):
                    self.send(half, second, step, slot)

    def relay(self, half, index):
        second = 1 - half
        step = 1 if index in RELAY_RIGHT else -1
        slot = self.place.slot(half, OFFSETS[index], -step)
        self.wait(half, slot)
        self.send(half, second, step, slot)

    def opposite(self):
        for half in (0, 1):
            self.relay(half, 0)
        for half in (0, 1):
            slot = self.place.slot(half, 2, 0)
            for part in (0, 1):
                self.wait(half, slot, part)
            for step in (1, -1):
                self.send(half, 1 - half, step, slot)

    def relays(self):
        for index in (1, 2, 3):
            for half in (0, 1):
                self.relay(half, index)

    def finish(self, half):
        for index in range(4):
            step = 1 if index in RELAY_RIGHT else -1
            self.wait(half, self.place.slot(half, OFFSETS[index], step))
            self.wait(half, self.place.slot(half, OFFSETS[index], 2))


class Scatter:
    def __init__(self, place, buf, relayed, left, right, mid, relayed2, left2, right2, sems, sems2, send_sems):
        self.place, self.buf = place, buf
        self.relayed, self.left, self.right = relayed, left, right
        self.mid, self.relayed2, self.left2, self.right2 = mid, relayed2, left2, right2
        self.sems, self.sems2, self.sends = sems, sems2, Sends(send_sems)

    def start(self):
        place = self.place
        for half in (0, 1):
            for way, (classes, step) in enumerate(((RELAY_RIGHT, 1), (RELAY_LEFT, -1))):
                for order, index in enumerate(classes):
                    self.sends.start(
                        self.buf.at[half, place.slot(half, 2, OFFSETS[index])],
                        self.relayed.at[half, way, order],
                        self.sems.at[half, 2, way * 2 + order],
                        place.along(half, step),
                    )
        for half in (0, 1):
            for index in RELAY_LEFT:
                self.sends.start(
                    self.buf.at[half, place.slot(half, 1, OFFSETS[index])],
                    self.left.at[half, index],
                    self.sems.at[half, 0, index],
                    place.along(half, 1),
                )
            for index in RELAY_RIGHT:
                self.sends.start(
                    self.buf.at[half, place.slot(half, -1, OFFSETS[index])],
                    self.right.at[half, index],
                    self.sems.at[half, 1, index],
                    place.along(half, -1),
                )

    def relays(self):
        place = self.place
        for order in (1, 0):
            for half in (0, 1):
                for way, (classes, step) in enumerate(((RELAY_RIGHT, 1), (RELAY_LEFT, -1))):
                    index = classes[order]
                    landed = self.relayed.at[half, way, order]
                    arrived(landed, self.sems.at[half, 2, way * 2 + order])
                    slot = place.slot(half, step, OFFSETS[index])
                    total = self.buf[half, slot].astype(F32) + landed[...].astype(F32)
                    self.buf[half, slot] = total.astype(BF16)
                    self.sends.start(
                        self.buf.at[half, slot],
                        (self.left if step == 1 else self.right).at[half, index],
                        self.sems.at[half, way, index],
                        place.along(half, step),
                    )

    def sums(self):
        place = self.place
        for index in (3, 1, 2, 0):
            for half in (0, 1):
                arrived(self.left.at[half, index], self.sems.at[half, 0, index])
                arrived(self.right.at[half, index], self.sems.at[half, 1, index])
                slot = place.slot(half, 0, OFFSETS[index])
                total = self.buf[half, slot].astype(F32) + self.left[half, index].astype(F32)
                total = total + self.right[half, index].astype(F32)
                self.mid[half, index] = total.astype(BF16)
                axis = 1 - half
                low, high = pl.ds(0, QUARTER), pl.ds(QUARTER, QUARTER)
                if index == 3:
                    for part, (cols, step) in enumerate(((low, 1), (high, -1))):
                        self.sends.start(
                            self.mid.at[half, 3, :, cols],
                            self.relayed2.at[half, part],
                            self.sems2.at[half, part],
                            place.along(axis, step),
                        )
                if index == 2:
                    self.sends.start(
                        self.mid.at[half, 2, :, high],
                        self.left2.at[half, :, high],
                        self.sems2.at[half, 2],
                        place.along(axis, 1),
                    )
                if index == 1:
                    self.sends.start(
                        self.mid.at[half, 1, :, low],
                        self.right2.at[half, :, low],
                        self.sems2.at[half, 3],
                        place.along(axis, -1),
                    )

    def last(self):
        place = self.place
        for half in (0, 1):
            axis = 1 - half
            for part, index, step, target in ((0, 2, 1, self.left2), (1, 1, -1, self.right2)):
                cols = pl.ds(part * QUARTER, QUARTER)
                arrived(self.relayed2.at[half, part], self.sems2.at[half, part])
                total = self.mid[half, index, :, cols].astype(F32) + self.relayed2[half, part].astype(F32)
                self.mid[half, index, :, cols] = total.astype(BF16)
                self.sends.start(
                    self.mid.at[half, index, :, cols],
                    target.at[half, :, cols],
                    self.sems2.at[half, 4 + part],
                    place.along(axis, step),
                )

    def result(self, half):
        low, high = pl.ds(0, QUARTER), pl.ds(QUARTER, QUARTER)
        arrived(self.left2.at[half, :, high], self.sems2.at[half, 2])
        arrived(self.right2.at[half, :, low], self.sems2.at[half, 3])
        arrived(self.left2.at[half, :, low], self.sems2.at[half, 4])
        arrived(self.right2.at[half, :, high], self.sems2.at[half, 5])
        total = self.mid[half, 0].astype(F32) + self.left2[half].astype(F32)
        return total + self.right2[half].astype(F32)

    def run(self):
        self.start()
        self.relays()
        self.sums()
        self.last()


class Handoff:
    def __init__(self, place, buf, sems, send_sems):
        self.place, self.buf, self.sems, self.sends = place, buf, sems, Sends(send_sems)

    def slot(self, step):
        return lax.rem(self.place.z + step + DEPTH, DEPTH) * 2 + self.place.core

    def piece(self, slot, part):
        if part is None:
            return self.buf.at[slot], self.sems.at[slot, 0]
        return self.buf.at[slot, :, pl.ds(part * HALF, HALF)], self.sems.at[slot, part]

    def send(self, slot, device, part=None):
        ref, sem = self.piece(slot, part)
        self.sends.start(ref, ref, sem, device)

    def wait(self, slot, part=None):
        ref, sem = self.piece(slot, part)
        arrived(ref, sem)

    def start(self):
        own = self.slot(0)
        for step in (1, -1):
            self.send(own, self.place.up(step))
        self.send(own, self.place.sibling())

    def step(self, number):
        for way in (1, -1):
            slot = self.slot(-way * number)
            if number < 4:
                self.wait(slot)
                part = None if number < 3 else (0 if way == 1 else 1)
                self.send(slot, self.place.up(way), part)
                self.send(slot, self.place.sibling())
        if number == 4:
            slot = self.slot(4)
            self.wait(slot, 0)
            self.wait(slot, 1)
            self.send(slot, self.place.sibling())

    def finish(self):
        for step in range(DEPTH):
            slot = lax.rem(self.place.z + step, DEPTH) * 2 + 1 - self.place.core
            self.wait(slot)


def kernel(
    prompt_ids,
    lengths,
    prompt_hbm,
    ctx_hbm,
    latent_hbm,
    imod_hbm,
    tmod_hbm,
    qkv_hbm,
    txt_hbm,
    gain,
    proj_hbm,
    out,
    prompt,
    ctx,
    latent,
    imod,
    tmod,
    qkv_w,
    txt_raw,
    txt_w,
    proj_w,
    local_sems,
    gathered,
    gather_sems,
    gather_sends,
    sc_buf,
    sc_relayed,
    sc_left,
    sc_right,
    sc_mid,
    sc_relayed2,
    sc_left2,
    sc_right2,
    sc_sems,
    sc_sems2,
    sc_sends,
    handed,
    hand_sems,
    hand_sends,
    x_state,
    text_in,
    text_kv,
    tscale,
):
    place = Place()

    loads = []

    def load(src, dst):
        copy = pltpu.make_async_copy(src, dst, local_sems.at[len(loads)])
        copy.start()
        loads.append(copy)
        return copy

    barrier = pltpu.get_barrier_semaphore()
    partners = [place.along(axis, step) for axis in (0, 1) for step in (1, -1)]
    partners += [place.up(1), place.up(-1), place.sibling()]
    for partner in partners:
        pl.semaphore_signal(barrier, inc=1, device_id=partner, device_id_type=MESH)

    load_prompt = load(prompt_hbm, prompt)
    load_ctx = load(ctx_hbm, ctx)
    load_latent = load(latent_hbm, latent)
    load_imod = load(imod_hbm, imod)
    load_tmod = load(tmod_hbm, tmod)
    load_qkv = [load(qkv_hbm.at[part], qkv_w.at[:, pl.ds(part * HEAD, HEAD)]) for part in range(3)]
    load_txt = load(txt_hbm, txt_raw)
    load_proj = load(proj_hbm, proj_w)

    bounds, running = [], 0
    for image in range(4):
        running = running + lengths[0, image]
        bounds.append(running)

    def segments_of(row_ids):
        return sum((row_ids >= bound).astype(jnp.int32) for bound in bounds)

    rows_iota = lax.broadcasted_iota(jnp.int32, (16 * ROWS, 1), 0)
    lanes_iota = lax.broadcasted_iota(jnp.int32, (1, 16 * ROWS), 1)
    mine = segments_of(place.tp * ROWS + lax.broadcasted_iota(jnp.int32, (ROWS, 1), 0))

    def modulation(step, kind, cols):
        rows = jnp.zeros((ROWS, cols.size), F32)
        for image in range(4):
            rows = jnp.where(mine == image, imod[image, kind, step : step + 1, cols], rows)
        return rows

    whole = pl.ds(0, WIDTH)
    halves = (pl.ds(0, HALF), pl.ds(HALF, HALF))

    def gather_of(which):
        return Gather(place, gathered.at[which], gather_sems.at[which], gather_sends.at[which])

    def scatter_of(which):
        return Scatter(
            place,
            *[
                ref.at[which]
                for ref in (
                    sc_buf,
                    sc_relayed,
                    sc_left,
                    sc_right,
                    sc_mid,
                    sc_relayed2,
                    sc_left2,
                    sc_right2,
                    sc_sems,
                    sc_sems2,
                    sc_sends,
                )
            ],
        )

    def put_block(which, values):
        for half in (0, 1):
            gathered[which, half, place.tp] = values[:, half * HALF : (half + 1) * HALF]

    load_prompt.wait()
    row = lax.broadcasted_iota(jnp.int32, (256, 256), 0)
    col = lax.broadcasted_iota(jnp.int32, (256, 256), 1)
    source = lax.rem(row // 4, 4) * 64 + (row // 16) * 4 + lax.rem(row, 4)
    order = (col == source).astype(BF16)
    ordered = jnp.dot(order, prompt[...], preferred_element_type=F32).astype(BF16)
    load_ctx.wait()

    def spread(which, left, weight_of):
        for half in (0, 1):
            for piece in range(HALF // 512):
                product = jnp.dot(left, weight_of(half * HALF + piece * 512), preferred_element_type=F32)
                sc_buf[which, half, :, :, pl.ds(piece * 512, 512)] = product.astype(BF16).reshape(16, ROWS, 512)

    spread(0, ordered, lambda at: ctx[:, pl.ds(at, 512)])

    pl.semaphore_wait(barrier, len(partners))
    text_scatter = scatter_of(0)
    text_scatter.start()

    load_latent.wait()
    load_imod.wait()
    x_state[...] = latent[...].astype(F32)

    def modulated(step):
        values = layer_norm(x_state[...])
        return (values * (1.0 + modulation(step, 1, whole)) + modulation(step, 0, whole)).astype(BF16)

    put_block(0, modulated(0))
    text_scatter.relays()
    text_scatter.sums()
    text_scatter.last()
    first_gather = gather_of(0)
    first_gather.start()

    handoff = Handoff(place, handed, hand_sems, hand_sends)
    for half in (0, 1):
        handed[place.group, :, halves[half]] = text_scatter.result(half).astype(BF16)
    handoff.start()
    first_gather.neighbours()
    handoff.step(1)
    first_gather.opposite()
    handoff.step(2)
    first_gather.relays()
    handoff.step(3)
    handoff.step(4)

    load_txt.wait()
    unweave = (col == lax.rem(row, 128) * 2 + row // 128).astype(BF16)

    def part_weights(chunk, carry):
        mixed = txt_raw[pl.ds(pl.multiple_of(chunk * 256, 256), 256), :]
        parted = jnp.dot(unweave, mixed, preferred_element_type=F32).astype(BF16)
        at = pl.ds(pl.multiple_of(chunk * 128, 128), 128)
        txt_w[at, 0:HEAD] = parted[:128]
        txt_w[at, HEAD:] = parted[128:]
        return carry

    lax.fori_loop(0, 24, part_weights, 0)

    load_tmod.wait()
    slot_image = lax.broadcasted_iota(jnp.int32, (ROWS, 1), 0) // 4
    for step in (0, 1):
        for kind in (0, 1):
            rows = jnp.zeros((ROWS, WIDTH), F32)
            for image in range(4):
                rows = jnp.where(slot_image == image, tmod[image, step, kind : kind + 1, :], rows)
            tscale[step, kind] = rows + float(kind)

    handoff.finish()
    pick_row = lax.broadcasted_iota(jnp.int32, (ROWS, 256), 0)
    pick_col = lax.broadcasted_iota(jnp.int32, (ROWS, 256), 1)
    wanted = jnp.zeros((ROWS, 256), jnp.int32)
    for image in range(4):
        wanted = jnp.where(pick_row // 4 == image, prompt_ids[place.group * 4 + image] * 4, wanted)
    pick = (pick_col == wanted + lax.rem(pick_row, 4)).astype(BF16)
    slot_text = jnp.concatenate(
        [
            jnp.dot(
                pick,
                handed[:, :, pl.ds(piece * 512, 512)].reshape(256, 512),
                preferred_element_type=F32,
            )
            for piece in range(6)
        ],
        axis=1,
    )
    put_block(2, layer_norm(slot_text).astype(BF16))
    text_gather = gather_of(2)
    text_gather.start()

    def project_image(which, gather):
        total = None
        for half in (0, 1):
            gather.finish(half)
            term = jnp.dot(
                gathered[which, half].reshape(256, HALF),
                qkv_w[pl.ds(half * HALF, HALF), :],
                preferred_element_type=F32,
            )
            total = term if total is None else total + term
        queries = rms_scale(total[:, :HEAD], gain[0:1]).astype(BF16)
        keys = rms_scale(total[:, HEAD : 2 * HEAD], gain[1:2]).astype(BF16)
        return queries, keys, total[:, 2 * HEAD :].astype(BF16)

    def project_text(step):
        for half in (0, 1):

            def modulate(owner, carry):
                normed = gathered[2, half, owner].astype(F32)
                scaled = normed * tscale[step, 1, :, halves[half]] + tscale[step, 0, :, halves[half]]
                text_in[half, owner] = scaled.astype(BF16)
                return carry

            lax.fori_loop(0, 16, modulate, 0)
        total = None
        for half in (0, 1):
            term = jnp.dot(
                text_in[half].reshape(256, HALF),
                txt_w[pl.ds(half * HALF, HALF), :],
                preferred_element_type=F32,
            )
            total = term if total is None else total + term
        text_kv[:, :HEAD] = rms_scale(total[:, :HEAD], gain[2:3]).astype(BF16)
        text_kv[:, HEAD:] = total[:, HEAD:].astype(BF16)

    segment_rows = segments_of(rows_iota)
    text_allowed = segment_rows == lax.rem(lanes_iota // 4, 4)
    image_allowed = segment_rows == segments_of(lanes_iota)

    def weigh(queries, keys, allowed):
        scores = lax.dot_general(queries, keys, (((1,), (1,)), ((), ())), preferred_element_type=F32)
        return jnp.where(allowed, jnp.exp(scores * HEAD**-0.5), 0.0)

    def attend(queries, keys, values):
        text_part = weigh(queries, text_kv[:, :HEAD], text_allowed)
        image_part = weigh(queries, keys, image_allowed)
        norm = jnp.sum(text_part, -1, keepdims=True) + jnp.sum(image_part, -1, keepdims=True)
        mixed = jnp.dot(text_part.astype(BF16), text_kv[:, HEAD:], preferred_element_type=F32)
        mixed = mixed + jnp.dot(image_part.astype(BF16), values, preferred_element_type=F32)
        return (mixed / norm).astype(BF16)

    def advance(step, scatter):
        for half in (0, 1):
            update = scatter.result(half)
            gate = modulation(step, 2, halves[half])
            state = x_state[:, halves[half]] + gate * update
            x_state[:, halves[half]] = state.astype(BF16).astype(F32)

    for copy in load_qkv:
        copy.wait()
    queries, keys, values = project_image(0, first_gather)
    text_gather.neighbours()
    text_gather.opposite()
    text_gather.relays()
    for half in (0, 1):
        text_gather.finish(half)
    project_text(0)
    load_proj.wait()

    def scatter_update(which, queries, keys, values):
        attended = attend(queries, keys, values)
        spread(which, attended, lambda at: proj_w[:, pl.ds(at, 512)])
        scatter = scatter_of(which)
        scatter.start()
        return scatter

    first_scatter = scatter_update(1, queries, keys, values)
    first_scatter.relays()
    project_text(1)
    first_scatter.sums()
    first_scatter.last()
    advance(0, first_scatter)

    put_block(1, modulated(1))
    second_gather = gather_of(1)
    second_gather.start()
    second_gather.neighbours()
    second_gather.opposite()
    second_gather.relays()
    queries, keys, values = project_image(1, second_gather)
    second_scatter = scatter_update(2, queries, keys, values)
    second_scatter.relays()
    second_scatter.sums()
    second_scatter.last()
    advance(1, second_scatter)
    out[...] = x_state[...].astype(BF16)

    for part in (text_scatter, first_gather, handoff, text_gather, first_scatter, second_gather, second_scatter):
        part.sends.finish()


def on_device(
    prompt_states,
    ctx_weight,
    image_prompt,
    image_lengths,
    latents,
    img_mod,
    txt_mod,
    img_qkv,
    txt_kv,
    qk_gain,
    img_proj,
):
    anywhere = pl.BlockSpec(memory_space=pl.ANY)
    scalars = pl.BlockSpec(memory_space=pltpu.SMEM)
    in_vmem = pl.BlockSpec(memory_space=pltpu.VMEM)
    dma = pltpu.SemaphoreType.DMA
    block = (ROWS, HALF)
    denoised = pl.pallas_call(
        kernel,
        out_shape=jax.ShapeDtypeStruct((ROWS, WIDTH), BF16),
        in_specs=[scalars, scalars] + [anywhere] * 7 + [in_vmem, anywhere],
        out_specs=in_vmem,
        scratch_shapes=[
            pltpu.VMEM((256, 256), BF16),
            pltpu.VMEM((256, WIDTH), BF16),
            pltpu.VMEM((ROWS, WIDTH), BF16),
            pltpu.VMEM((4, 3, 2, WIDTH), F32),
            pltpu.VMEM((4, 2, 2, WIDTH), F32),
            pltpu.VMEM((WIDTH, 3 * HEAD), BF16),
            pltpu.VMEM((2 * WIDTH, HEAD), BF16),
            pltpu.VMEM((WIDTH, 2 * HEAD), BF16),
            pltpu.VMEM((HEAD, WIDTH), BF16),
            dma((10,)),
            pltpu.VMEM((3, 2, 16) + block, BF16),
            dma((3, 2, 16, 2)),
            dma((3, 36)),
            pltpu.VMEM((3, 2, 16) + block, BF16),
            pltpu.VMEM((3, 2, 2, 2) + block, BF16),
            pltpu.VMEM((3, 2, 4) + block, BF16),
            pltpu.VMEM((3, 2, 4) + block, BF16),
            pltpu.VMEM((3, 2, 4) + block, BF16),
            pltpu.VMEM((3, 2, 2, ROWS, QUARTER), BF16),
            pltpu.VMEM((3, 2) + block, BF16),
            pltpu.VMEM((3, 2) + block, BF16),
            dma((3, 2, 3, 4)),
            dma((3, 2, 6)),
            dma((3, 36)),
            pltpu.VMEM((16, ROWS, WIDTH), BF16),
            dma((16, 2)),
            dma((24,)),
            pltpu.VMEM((ROWS, WIDTH), F32),
            pltpu.VMEM((2, 16) + block, BF16),
            pltpu.VMEM((256, 2 * HEAD), BF16),
            pltpu.VMEM((2, 2, ROWS, WIDTH), F32),
        ],
        compiler_params=pltpu.CompilerParams(
            collective_id=0, has_side_effects=True, vmem_limit_bytes=56 * 1024 * 1024
        ),
    )(
        image_prompt,
        image_lengths,
        prompt_states.reshape(256, 256),
        ctx_weight,
        latents[0],
        jnp.transpose(img_mod[0], (0, 2, 1, 3)),
        txt_mod[0],
        jnp.transpose(img_qkv, (1, 0, 2)),
        txt_kv.reshape(2 * WIDTH, HEAD),
        qk_gain,
        img_proj,
    )
    return denoised[None]


def solution(mesh):
    placed = (
        P("group", None, "tp"),
        P("tp", None),
        P(),
        P("group", None),
        P("group", "tp", None),
        P("group", None, None, None, None),
        P("group", None, None, None, None),
        P(None, None, "tp"),
        P(None, None, "tp"),
        P(),
        P("tp", None),
    )
    return jax.shard_map(
        on_device, mesh=mesh, in_specs=placed, out_specs=P("group", "tp", None), check_vma=False
    )
```

time: 473 us -> 118 us (0.25)
  waiting for transfers between devices: 415 us -> 0 us
  Pallas kernels: 0 us -> 116 us
  matrix products: 26 us -> 0 us
  between operations: 13.9 us -> 0.01 us
  local copies, waits for them, and re-layouts: 9.65 us -> 1.54 us
  other arithmetic: 7.93 us -> 0 us
    reduce_scatter x3 -> x0, waiting for transfers between devices: 239 us -> none  [the longest x2 156 us: on_device(): lax.psum_scatter(jnp.dot(attended, img_proj, preferred_element_type=jnp.f...]
    all_gather x4 -> x0, waiting for transfers between devices: 176 us -> none  [the longest x2 94.7 us: on_device(): piece_rows = lax.all_gather(modulated, 'tp', axis=0, tiled=True)]
    pallas_call x0 -> x1, Pallas kernels: none -> 116 us  [on_device(): pl.pallas_call(kernel, out_shape=jax.ShapeDtypeStruct((ROWS, WIDTH), BF16...]
    dot_general x15 -> x0, matrix products: 26 us -> none  [the longest x6 7.17 us: per_row(): return jnp.dot(onehot, mod_table, precision=lax.Precision.HIGHEST)]
  transfers between devices with their start and end apart: 7 -> 0, of which waited for: 7 -> 0; matrix products, arithmetic and copies ran while one was open for 2% -> 0% of each run, Pallas kernels for 0% -> 0%
where the time goes in v1:
time: 118 us; the launch traced here: 117 us
  Pallas kernels  116 us (98%)
  local copies, waits for them, and re-layouts  1.54 us (1%)
    pallas_call x1, Pallas kernels, on_device(): pl.pallas_call(kernel, out_shape=jax.ShapeDtypeStruct((ROWS, WIDTH), BF16...  116 us

profile of v1, /device:TPU:32, one launch (start us, length us, event | category | flops | bytes accessed | tf_op | source)
XLA Modules:
  0.0 117.3 jit_solution(12150935341394536238)
XLA Ops:
  0.0 115.7 %shard_map.109 = bf16[16,3072]{1,0:T(8,128)(2,1)} custom-call(s32[64]{0:T(128)} %prompt_ids.1, s32[1,4]{1,0:T(1,128)} %lengths.1, bf16[256,256]{1,0:T(8,128)(2,1)} %bitcast.14, bf16[256,3072]{1,0:T(8,128)(2,1)} %ctx_hbm.1, bf16[16,3072]{1,0:T(8,128)(2,1)} %bitcast.15, f32[4,3,2,3072]{3,2,1,0:T(2,128)} %bitcast.12, f32[4,2,2,3072]{3,2,1,0:T(2,128)} %bitcast.13, ...), custom_call_target="tpu_custom_call" | custom-call | tf_op jit(solution)/shard_map/pallas_call | solution.py:641
  115.8 1.5 %copy.13 = bf16[1,16,3072]{2,1,0:T(8,128)(2,1)} copy(bf16[1,16,3072]{2,1,0:T(8,128)(2,1)} %bitcast.11) | data formatting | bytes 196608

commit v2 on v0

v2 whole, which is shorter than its diff:
```python
import functools

import jax
import jax.numpy as jnp
from jax import lax
from jax.experimental import pallas as pl
from jax.experimental.pallas import tpu as pltpu
from jax.sharding import PartitionSpec as P

MESH = pl.DeviceIdType.MESH
F32, BF16 = jnp.float32, jnp.bfloat16
WIDTH, HALF = 3072, 1536
ROWS = 16
SIDE = 4
DEPTH = 8
HEAD = 128
STEPS = (1, -1, 2)


def layer_norm(values):
    centered = values - jnp.mean(values, -1, keepdims=True)
    return centered * lax.rsqrt(jnp.mean(centered * centered, -1, keepdims=True) + 1e-6)


def rms_scale(values, gain_row):
    return values * lax.rsqrt(jnp.mean(values * values, -1, keepdims=True) + 1e-6) * gain_row


class Place:
    def __init__(self):
        self.group, self.tp = lax.axis_index("group"), lax.axis_index("tp")
        self.x, self.y = lax.rem(self.tp, SIDE), self.tp // SIDE
        self.z, self.core = self.group // 2, lax.rem(self.group, 2)

    def along(self, axis, step):
        if axis == 0:
            return (self.group, self.y * SIDE + lax.rem(self.x + step + SIDE, SIDE))
        return (self.group, lax.rem(self.y + step + SIDE, SIDE) * SIDE + self.x)

    def slot(self, half, first, second):
        dx, dy = (first, second) if half == 0 else (second, first)
        return lax.rem(self.y + dy + SIDE, SIDE) * SIDE + lax.rem(self.x + dx + SIDE, SIDE)

    def up(self, step):
        return (lax.rem(self.z + step + DEPTH, DEPTH) * 2 + self.core, self.tp)

    def sibling(self):
        return (self.z * 2 + 1 - self.core, self.tp)


def await_bytes(ref, sem):
    pltpu.make_async_copy(ref, ref, sem).wait()


def push(src, dst, send, recv, device):
    pltpu.make_async_remote_copy(
        src_ref=src, dst_ref=dst, send_sem=send, recv_sem=recv, device_id=device, device_id_type=MESH
    ).start()


class Gather:
    def __init__(self, place, buf, sems, send, pieces):
        self.place, self.buf, self.sems, self.send, self.pieces = place, buf, sems, send, pieces

    def cols(self, piece):
        return pl.ds(piece * (HALF // self.pieces), HALF // self.pieces)

    def pass_on(self, piece, half, slot, axis, base):
        ref = self.buf.at[half, slot, :, self.cols(piece)]
        for index, step in enumerate(STEPS):
            push(ref, ref, self.send, self.sems.at[piece, half, base + index], self.place.along(axis, step))

    def start(self, piece):
        for base in (0, 3):
            for half in (0, 1):
                own = self.place.slot(half, 0, 0)
                self.pass_on(piece, half, own, half if base == 0 else 1 - half, base)

    def forward(self, piece):
        for index, step in enumerate(STEPS):
            for half in (0, 1):
                slot = self.place.slot(half, -step, 0)
                await_bytes(self.buf.at[half, slot, :, self.cols(piece)], self.sems.at[piece, half, index])
                self.pass_on(piece, half, slot, 1 - half, 3)

    def finish(self, piece, half):
        for index in range(3):
            await_bytes(self.buf.at[half, pl.ds(0, 4), :, self.cols(piece)], self.sems.at[piece, half, 3 + index])

    def close(self):
        await_bytes(self.buf.at[:, pl.ds(0, 15)], self.send)


class Scatter:
    def __init__(self, place, buf, landed, mid, own, landed2, sems, send, pieces):
        self.place, self.buf, self.landed, self.mid = place, buf, landed, mid
        self.own, self.landed2, self.sems, self.send, self.pieces = own, landed2, sems, send, pieces

    def cols(self, piece):
        return pl.ds(piece * (HALF // self.pieces), HALF // self.pieces)

    def at(self, half, first, second):
        a, b = (self.place.x, self.place.y) if half == 0 else (self.place.y, self.place.x)
        return lax.rem(a + first + SIDE, SIDE), lax.rem(b + second + SIDE, SIDE)

    def start(self, piece):
        for order, second in enumerate((2, 1, -1, 0)):
            for half in (0, 1):
                for index, step in enumerate(STEPS):
                    one, two = self.at(half, step, second)
                    push(
                        self.buf.at[half, one, two, :, self.cols(piece)],
                        self.landed.at[half, index, order, :, self.cols(piece)],
                        self.send.at[0],
                        self.sems.at[piece, half, order],
                        self.place.along(half, step),
                    )

    def sums(self, piece):
        cols = self.cols(piece)
        for order, second in enumerate((2, 1, -1, 0)):
            for half in (0, 1):
                await_bytes(self.landed.at[half, :, order, :, cols], self.sems.at[piece, half, order])
                one, two = self.at(half, 0, second)
                total = self.buf[half, one, two, :, cols].astype(F32)
                for index in range(3):
                    total = total + self.landed[half, index, order, :, cols].astype(F32)
                if second == 0:
                    self.own[half, :, cols] = total
                else:
                    self.mid[half, order, :, cols] = total.astype(BF16)
                    push(
                        self.mid.at[half, order, :, cols],
                        self.landed2.at[half, order, :, cols],
                        self.send.at[1],
                        self.sems.at[piece, half, 4],
                        self.place.along(1 - half, second),
                    )

    def result(self, piece, half):
        cols = self.cols(piece)
        await_bytes(self.landed2.at[half, :, :, cols], self.sems.at[piece, half, 4])
        total = self.own[half, :, cols]
        for index in range(3):
            total = total + self.landed2[half, index, :, cols].astype(F32)
        return total

    def close(self):
        await_bytes(self.buf.at[:, pl.ds(0, 3)], self.send.at[0])
        await_bytes(self.mid, self.send.at[1])


class Handoff:
    def __init__(self, place, buf, sems, sibling_sem, send, pieces):
        self.place, self.buf, self.sems, self.sibling_sem = place, buf, sems, sibling_sem
        self.send, self.pieces = send, pieces

    def slot(self, step):
        return lax.rem(self.place.z + step + DEPTH, DEPTH) * 2 + self.place.core

    def piece(self, slot, piece):
        return self.buf.at[slot, :, pl.ds(piece * (WIDTH // self.pieces), WIDTH // self.pieces)]

    def carries(self, number, piece, side):
        return number < 4 or (piece >= self.pieces // 2) == (side == 1)

    def onward(self, number, piece, side):
        way = (1, -1)[side]
        ref = self.piece(self.slot(-way * number), piece)
        push(ref, ref, self.send, self.sems.at[number, piece, side], self.place.up(way))

    def across(self, slot):
        ref = self.buf.at[slot]
        push(ref, ref, self.send, self.sibling_sem, self.place.sibling())

    def start(self, piece):
        for side in (0, 1):
            self.onward(0, piece, side)

    def step(self, number, piece):
        for side in (0, 1):
            if self.carries(number, piece, side):
                slot = self.slot(-(1, -1)[side] * number)
                await_bytes(self.piece(slot, piece), self.sems.at[number - 1, piece, side])
                if number < 4 and self.carries(number + 1, piece, side):
                    self.onward(number, piece, side)

    def share(self, number):
        if number == 0 or number == 4:
            self.across(self.slot(number))
        else:
            self.across(self.slot(number))
            self.across(self.slot(-number))

    def finish(self):
        await_bytes(self.buf.at[pl.ds(0, DEPTH)], self.sibling_sem)

    def close(self):
        await_bytes(self.buf.at[pl.ds(0, 15)], self.send)


class Update:
    def __init__(self, place, weights, outgoing, incoming, products, landed, sems, send):
        self.place, self.weights, self.outgoing, self.incoming = place, weights, outgoing, incoming
        self.products, self.landed, self.sems, self.send = products, landed, sems, send

    def positions(self, half):
        return (self.place.x, self.place.y) if half == 0 else (self.place.y, self.place.x)

    def start(self, attended):
        blocks = attended.reshape(SIDE, SIDE, ROWS, HEAD)
        self.outgoing[0] = blocks
        for one in range(SIDE):
            for two in range(SIDE):
                self.outgoing[1, one, two] = blocks[two, one]
        for half in (0, 1):
            second = self.positions(half)[1]
            for step in (2, 1, -1):
                push(
                    self.outgoing.at[half, lax.rem(second + step + SIDE, SIDE)],
                    self.incoming.at[half, second],
                    self.send.at[0],
                    self.sems.at[half, 0],
                    self.place.along(1 - half, step),
                )
            self.incoming[half, second] = self.outgoing[half, second]

    def multiply(self):
        for half in (0, 1):
            first = self.positions(half)[0]
            await_bytes(self.incoming.at[half, pl.ds(0, 3)], self.sems.at[half, 0])
            left = jnp.concatenate([self.incoming[half, other].reshape(4 * ROWS, HEAD) for other in range(SIDE)], 1)
            for piece in range(3):
                cols = pl.ds(piece * 512, 512)
                right = self.weights[half, :, :, :, cols].reshape(SIDE * HEAD, 512)
                product = jnp.dot(left, right, preferred_element_type=F32)
                self.products[half, :, :, cols] = product.astype(BF16).reshape(SIDE, ROWS, 512)
            for index, step in enumerate(STEPS):
                push(
                    self.products.at[half, lax.rem(first + step + SIDE, SIDE)],
                    self.landed.at[half, index],
                    self.send.at[1],
                    self.sems.at[half, 1],
                    self.place.along(half, step),
                )

    def result(self, half):
        first = self.positions(half)[0]
        await_bytes(self.landed.at[half], self.sems.at[half, 1])
        total = self.products[half, first].astype(F32)
        for index in range(3):
            total = total + self.landed[half, index].astype(F32)
        return total

    def close(self):
        await_bytes(self.outgoing.at[:, pl.ds(0, 3)], self.send.at[0])
        await_bytes(self.landed, self.send.at[1])


class ProjectionWeights:
    def __init__(self, place, buf, sems, sibling_sem, send):
        self.place, self.buf, self.sems, self.sibling_sem, self.send = place, buf, sems, sibling_sem, send

    def second(self, half, step):
        return lax.rem((self.place.y if half == 0 else self.place.x) + step + SIDE, SIDE)

    def start(self):
        for step_index, step in enumerate(STEPS):
            for half in (0, 1):
                ref = self.buf.at[half, self.second(half, 0), self.place.core]
                push(ref, ref, self.send, self.sems.at[half, step_index], self.place.along(1 - half, step))

    def share(self):
        for index, step in enumerate(STEPS):
            for half in (0, 1):
                ref = self.buf.at[half, self.second(half, -step), self.place.core]
                await_bytes(ref, self.sems.at[half, index])
                push(ref, ref, self.send, self.sibling_sem, self.place.sibling())

    def finish(self):
        await_bytes(self.buf.at[0, pl.ds(0, 3)], self.sibling_sem)

    def close(self):
        await_bytes(self.buf.at[:, pl.ds(0, 3)], self.send)


def kernel(
    prompt_ids,
    lengths,
    prompt_hbm,
    ctx_hbm,
    latent_hbm,
    imod_hbm,
    tmod_hbm,
    qkv_hbm,
    txt_hbm,
    gain,
    proj_hbm,
    out,
    prompt,
    ctx,
    latent,
    imod,
    tmod,
    qkv_w,
    txt_raw,
    txt_w,
    proj_w,
    local_sems,
    proj_sems,
    proj_sibling,
    proj_send,
    gathered,
    gather_sems,
    gather_sends,
    sc_buf,
    sc_landed,
    sc_mid,
    sc_own,
    sc_landed2,
    sc_sems,
    sc_sends,
    handed,
    hand_sems,
    hand_sibling,
    hand_send,
    up_outgoing,
    up_incoming,
    up_products,
    up_landed,
    up_sems,
    up_sends,
    x_state,
    rows_mod,
    text_in,
    text_kv,
    tscale,
):
    place = Place()

    barrier = pltpu.get_barrier_semaphore()
    partners = [place.along(axis, step) for axis in (0, 1) for step in STEPS]
    partners += [place.up(1), place.up(-1), place.sibling()]
    for partner in partners:
        pl.semaphore_signal(barrier, inc=1, device_id=partner, device_id_type=MESH)

    loads = []

    def load(src, dst):
        copy = pltpu.make_async_copy(src, dst, local_sems.at[len(loads)])
        copy.start()
        loads.append(copy)
        return copy

    load_prompt = load(prompt_hbm, prompt)
    load_ctx = load(ctx_hbm, ctx)
    load_latent = load(latent_hbm, latent)
    load_imod = load(imod_hbm, imod)
    load_proj = [
        load(
            proj_hbm.at[pl.ds(share * 64, 64), pl.ds(half * HALF, HALF)],
            proj_w.at[half, place.y if half == 0 else place.x, share],
        )
        for half in (0, 1)
        for share in (0, 1)
    ]
    load_txt = load(txt_hbm, txt_raw)
    load_tmod = load(tmod_hbm, tmod)
    load_qkv = [load(qkv_hbm.at[part], qkv_w.at[:, pl.ds(part * HEAD, HEAD)]) for part in range(3)]

    bounds, running = [], 0
    for image in range(4):
        running = running + lengths[0, image]
        bounds.append(running)

    def segments_of(row_ids):
        return sum((row_ids >= bound).astype(jnp.int32) for bound in bounds)

    rows_iota = lax.broadcasted_iota(jnp.int32, (16 * ROWS, 1), 0)
    lanes_iota = lax.broadcasted_iota(jnp.int32, (1, 16 * ROWS), 1)
    halves = (pl.ds(0, HALF), pl.ds(HALF, HALF))

    load_prompt.wait()
    row = lax.broadcasted_iota(jnp.int32, (256, 256), 0)
    col = lax.broadcasted_iota(jnp.int32, (256, 256), 1)
    ordered = []
    for half in (0, 1):
        block = row // 16
        owner = block if half == 1 else lax.rem(block, 4) * 4 + block // 4
        source = lax.rem(row // 4, 4) * 64 + owner * 4 + lax.rem(row, 4)
        order = (col == source).astype(BF16)
        ordered.append(jnp.dot(order, prompt[...], preferred_element_type=F32).astype(BF16))
    load_ctx.wait()
    for half in (0, 1):
        for piece in range(3):
            weight = ctx[:, pl.ds(half * HALF + piece * 512, 512)]
            product = jnp.dot(ordered[half], weight, preferred_element_type=F32)
            sc_buf[half, :, :, :, pl.ds(piece * 512, 512)] = product.astype(BF16).reshape(4, 4, ROWS, 512)

    pl.semaphore_wait(barrier, len(partners))
    text_scatter = Scatter(place, sc_buf, sc_landed, sc_mid, sc_own, sc_landed2, sc_sems, sc_sends, 1)
    text_scatter.start(0)

    load_imod.wait()
    mine = segments_of(place.tp * ROWS + lax.broadcasted_iota(jnp.int32, (ROWS, 1), 0))
    for step in (0, 1):
        for kind in range(3):
            rows = jnp.zeros((ROWS, WIDTH), F32)
            for image in range(4):
                rows = jnp.where(mine == image, imod[image, kind, step : step + 1, :], rows)
            rows_mod[step, kind] = rows + 1.0 if kind == 1 else rows
    load_latent.wait()
    x_state[...] = latent[...].astype(F32)

    def put_block(which, values):
        for half in (0, 1):
            gathered[which, half, place.tp] = values[:, half * HALF : (half + 1) * HALF]

    def put_image(step):
        values = layer_norm(x_state[...])
        put_block(step, (values * rows_mod[step, 1] + rows_mod[step, 0]).astype(BF16))

    def gather_of(which):
        return Gather(place, gathered.at[which], gather_sems.at[which], gather_sends.at[which], 1)

    put_image(0)
    text_scatter.sums(0)
    first_gather = gather_of(0)
    first_gather.start(0)

    handoff = Handoff(place, handed, hand_sems, hand_sibling, hand_send, 2)
    for half in (0, 1):
        handed[place.group, :, halves[half]] = text_scatter.result(0, half).astype(BF16)
        handoff.start(half)
    handoff.share(0)

    def hand_step(number):
        for piece in (0, 1):
            handoff.step(number, piece)
        handoff.share(number)

    first_gather.forward(0)
    hand_step(1)
    for copy in load_proj:
        copy.wait()
    weights = ProjectionWeights(place, proj_w, proj_sems, proj_sibling, proj_send)
    weights.start()

    load_txt.wait()
    unweave = (col == lax.rem(row, 128) * 2 + row // 128).astype(BF16)

    def part_weights(chunk, carry):
        mixed = txt_raw[pl.ds(pl.multiple_of(chunk * 256, 256), 256), :]
        parted = jnp.dot(unweave, mixed, preferred_element_type=F32).astype(BF16)
        at = pl.ds(pl.multiple_of(chunk * 128, 128), 128)
        txt_w[at, 0:HEAD] = parted[:128]
        txt_w[at, HEAD:] = parted[128:]
        return carry

    lax.fori_loop(0, 12, part_weights, 0)
    hand_step(2)
    lax.fori_loop(12, 24, part_weights, 0)
    hand_step(3)

    load_tmod.wait()
    slot_image = lax.broadcasted_iota(jnp.int32, (ROWS, 1), 0) // 4
    for step in (0, 1):
        for kind in (0, 1):
            rows = jnp.zeros((ROWS, WIDTH), F32)
            for image in range(4):
                rows = jnp.where(slot_image == image, tmod[image, step, kind : kind + 1, :], rows)
            tscale[step, kind] = rows + float(kind)
    hand_step(4)

    pick_row = lax.broadcasted_iota(jnp.int32, (ROWS, 256), 0)
    pick_col = lax.broadcasted_iota(jnp.int32, (ROWS, 256), 1)
    wanted = jnp.zeros((ROWS, 256), jnp.int32)
    for image in range(4):
        wanted = jnp.where(pick_row // 4 == image, prompt_ids[place.group * 4 + image] * 4, wanted)
    pick = (pick_col == wanted + lax.rem(pick_row, 4)).astype(BF16)
    handoff.finish()
    slot_text = jnp.concatenate(
        [
            jnp.dot(
                pick,
                handed[:, :, pl.ds(piece * 512, 512)].reshape(256, 512),
                preferred_element_type=F32,
            )
            for piece in range(6)
        ],
        axis=1,
    )
    put_block(2, layer_norm(slot_text).astype(BF16))
    text_gather = gather_of(2)
    text_gather.start(0)

    def project_image(which, gather):
        total = None
        for half in (0, 1):
            gather.finish(0, half)
            term = jnp.dot(
                gathered[which, half].reshape(256, HALF),
                qkv_w[pl.ds(half * HALF, HALF), :],
                preferred_element_type=F32,
            )
            total = term if total is None else total + term
        queries = rms_scale(total[:, :HEAD], gain[0:1]).astype(BF16)
        keys = rms_scale(total[:, HEAD : 2 * HEAD], gain[1:2]).astype(BF16)
        return queries, keys, total[:, 2 * HEAD :].astype(BF16)

    def project_text(step):
        for half in (0, 1):

            def modulate(owner, carry):
                normed = gathered[2, half, owner].astype(F32)
                scaled = normed * tscale[step, 1, :, halves[half]] + tscale[step, 0, :, halves[half]]
                text_in[half, owner] = scaled.astype(BF16)
                return carry

            lax.fori_loop(0, 16, modulate, 0)
        total = None
        for half in (0, 1):
            term = jnp.dot(
                text_in[half].reshape(256, HALF),
                txt_w[pl.ds(half * HALF, HALF), :],
                preferred_element_type=F32,
            )
            total = term if total is None else total + term
        text_kv[:, :HEAD] = rms_scale(total[:, :HEAD], gain[2:3]).astype(BF16)
        text_kv[:, HEAD:] = total[:, HEAD:].astype(BF16)

    segment_rows = segments_of(rows_iota)
    text_allowed = segment_rows == lax.rem(lanes_iota // 4, 4)
    image_allowed = segment_rows == segments_of(lanes_iota)

    def weigh(queries, keys, allowed):
        scores = lax.dot_general(queries, keys, (((1,), (1,)), ((), ())), preferred_element_type=F32)
        return jnp.where(allowed, jnp.exp(scores * HEAD**-0.5), 0.0)

    def attend(queries, keys, values):
        text_part = weigh(queries, text_kv[:, :HEAD], text_allowed)
        image_part = weigh(queries, keys, image_allowed)
        norm = jnp.sum(text_part, -1, keepdims=True) + jnp.sum(image_part, -1, keepdims=True)
        mixed = jnp.dot(text_part.astype(BF16), text_kv[:, HEAD:], preferred_element_type=F32)
        mixed = mixed + jnp.dot(image_part.astype(BF16), values, preferred_element_type=F32)
        return (mixed / norm).astype(BF16)

    def update_of(which):
        parts = (up_outgoing, up_incoming, up_products, up_landed, up_sems, up_sends)
        return Update(place, proj_w, *[ref.at[which] for ref in parts])

    def advance(step, update):
        for half in (0, 1):
            gate = rows_mod[step, 2, :, halves[half]]
            state = x_state[:, halves[half]] + gate * update.result(half)
            x_state[:, halves[half]] = state.astype(BF16).astype(F32)

    weights.share()
    text_gather.forward(0)
    for copy in load_qkv:
        copy.wait()
    queries, keys, values = project_image(0, first_gather)
    weights.finish()
    for half in (0, 1):
        text_gather.finish(0, half)
    project_text(0)

    first_update = update_of(0)
    first_update.start(attend(queries, keys, values))
    first_update.multiply()
    project_text(1)
    advance(0, first_update)

    put_image(1)
    second_gather = gather_of(1)
    second_gather.start(0)
    second_gather.forward(0)
    queries, keys, values = project_image(1, second_gather)
    second_update = update_of(1)
    second_update.start(attend(queries, keys, values))
    second_update.multiply()
    advance(1, second_update)
    out[...] = x_state[...].astype(BF16)

    for part in (text_scatter, first_gather, handoff, weights, text_gather, first_update, second_gather, second_update):
        part.close()


def on_device(
    prompt_states,
    ctx_weight,
    image_prompt,
    image_lengths,
    latents,
    img_mod,
    txt_mod,
    img_qkv,
    txt_kv,
    qk_gain,
    img_proj,
):
    anywhere = pl.BlockSpec(memory_space=pl.ANY)
    scalars = pl.BlockSpec(memory_space=pltpu.SMEM)
    in_vmem = pl.BlockSpec(memory_space=pltpu.VMEM)
    dma = pltpu.SemaphoreType.DMA
    block = (ROWS, HALF)
    denoised = pl.pallas_call(
        kernel,
        out_shape=jax.ShapeDtypeStruct((ROWS, WIDTH), BF16),
        in_specs=[scalars, scalars] + [anywhere] * 7 + [in_vmem, anywhere],
        out_specs=in_vmem,
        scratch_shapes=[
            pltpu.VMEM((256, 256), BF16),
            pltpu.VMEM((256, WIDTH), BF16),
            pltpu.VMEM((ROWS, WIDTH), BF16),
            pltpu.VMEM((4, 3, 2, WIDTH), F32),
            pltpu.VMEM((4, 2, 2, WIDTH), F32),
            pltpu.VMEM((WIDTH, 3 * HEAD), BF16),
            pltpu.VMEM((2 * WIDTH, HEAD), BF16),
            pltpu.VMEM((WIDTH, 2 * HEAD), BF16),
            pltpu.VMEM((2, 4, 2, 64, HALF), BF16),
            dma((13,)),
            dma((2, 3)),
            dma,
            dma,
            pltpu.VMEM((3, 2, 16) + block, BF16),
            dma((3, 1, 2, 6)),
            dma((3,)),
            pltpu.VMEM((2, 4, 4) + block, BF16),
            pltpu.VMEM((2, 3, 4) + block, BF16),
            pltpu.VMEM((2, 3) + block, BF16),
            pltpu.VMEM((2,) + block, F32),
            pltpu.VMEM((2, 3) + block, BF16),
            dma((1, 2, 5)),
            dma((2,)),
            pltpu.VMEM((16, ROWS, WIDTH), BF16),
            dma((4, 2, 2)),
            dma,
            dma,
            pltpu.VMEM((2, 2, 4, 4, ROWS, HEAD), BF16),
            pltpu.VMEM((2, 2, 4, 4, ROWS, HEAD), BF16),
            pltpu.VMEM((2, 2, 4) + block, BF16),
            pltpu.VMEM((2, 2, 3) + block, BF16),
            dma((2, 2, 2)),
            dma((2, 2)),
            pltpu.VMEM((ROWS, WIDTH), F32),
            pltpu.VMEM((2, 3, ROWS, WIDTH), F32),
            pltpu.VMEM((2, 16) + block, BF16),
            pltpu.VMEM((256, 2 * HEAD), BF16),
            pltpu.VMEM((2, 2, ROWS, WIDTH), F32),
        ],
        compiler_params=pltpu.CompilerParams(
            collective_id=0, has_side_effects=True, vmem_limit_bytes=56 * 1024 * 1024
        ),
    )(
        image_prompt,
        image_lengths,
        prompt_states.reshape(256, 256),
        ctx_weight,
        latents[0],
        jnp.transpose(img_mod[0], (0, 2, 1, 3)),
        txt_mod[0],
        jnp.transpose(img_qkv, (1, 0, 2)),
        txt_kv.reshape(2 * WIDTH, HEAD),
        qk_gain,
        img_proj,
    )
    return denoised[None]


def solution(mesh):
    placed = (
        P("group", None, "tp"),
        P("tp", None),
        P(),
        P("group", None),
        P("group", "tp", None),
        P("group", None, None, None, None),
        P("group", None, None, None, None),
        P(None, None, "tp"),
        P(None, None, "tp"),
        P(),
        P("tp", None),
    )
    return jax.shard_map(
        on_device, mesh=mesh, in_specs=placed, out_specs=P("group", "tp", None), check_vma=False
    )
```

time: 473 us -> 89.3 us (0.19)
  waiting for transfers between devices: 415 us -> 0 us
  Pallas kernels: 0 us -> 87.6 us
  matrix products: 26 us -> 0 us
  between operations: 13.9 us -> 0.01 us
  local copies, waits for them, and re-layouts: 9.65 us -> 1.54 us
  other arithmetic: 7.93 us -> 0 us
    reduce_scatter x3 -> x0, waiting for transfers between devices: 239 us -> none  [the longest x2 156 us: on_device(): lax.psum_scatter(jnp.dot(attended, img_proj, preferred_element_type=jnp.f...]
    all_gather x4 -> x0, waiting for transfers between devices: 176 us -> none  [the longest x2 94.7 us: on_device(): piece_rows = lax.all_gather(modulated, 'tp', axis=0, tiled=True)]
    pallas_call x0 -> x1, Pallas kernels: none -> 87.6 us  [on_device(): pl.pallas_call(kernel, out_shape=jax.ShapeDtypeStruct((ROWS, WIDTH), BF16...]
    dot_general x15 -> x0, matrix products: 26 us -> none  [the longest x6 7.17 us: per_row(): return jnp.dot(onehot, mod_table, precision=lax.Precision.HIGHEST)]
  transfers between devices with their start and end apart: 7 -> 0, of which waited for: 7 -> 0; matrix products, arithmetic and copies ran while one was open for 2% -> 0% of each run, Pallas kernels for 0% -> 0%
where the time goes in v2:
time: 89.3 us; the launch traced here: 89.1 us
  Pallas kernels  87.6 us (98%)
  local copies, waits for them, and re-layouts  1.54 us (2%)
    pallas_call x1, Pallas kernels, on_device(): pl.pallas_call(kernel, out_shape=jax.ShapeDtypeStruct((ROWS, WIDTH), BF16...  87.6 us

profile of v2, /device:TPU:32, one launch (start us, length us, event | category | flops | bytes accessed | tf_op | source)
XLA Modules:
  0.0 89.1 jit_solution(4202139122423442813)
XLA Ops:
  0.0 87.6 %shard_map.109 = bf16[16,3072]{1,0:T(8,128)(2,1)} custom-call(s32[64]{0:T(128)} %prompt_ids.1, s32[1,4]{1,0:T(1,128)} %lengths.1, bf16[256,256]{1,0:T(8,128)(2,1)} %bitcast.14, bf16[256,3072]{1,0:T(8,128)(2,1)} %ctx_hbm.1, bf16[16,3072]{1,0:T(8,128)(2,1)} %bitcast.15, f32[4,3,2,3072]{3,2,1,0:T(2,128)} %bitcast.12, f32[4,2,2,3072]{3,2,1,0:T(2,128)} %bitcast.13, ...), custom_call_target="tpu_custom_call" | custom-call | tf_op jit(solution)/shard_map/pallas_call | solution.py:607
  87.6 1.5 %copy.13 = bf16[1,16,3072]{2,1,0:T(8,128)(2,1)} copy(bf16[1,16,3072]{2,1,0:T(8,128)(2,1)} %bitcast.11) | data formatting | bytes 196608

commit v3 on v2

--- a/solution.py
+++ b/solution.py
@@ -9,12 +9,14 @@
 
 MESH = pl.DeviceIdType.MESH
 F32, BF16 = jnp.float32, jnp.bfloat16
-WIDTH, HALF = 3072, 1536
+WIDTH, HALF, QUARTER = 3072, 1536, 768
 ROWS = 16
 SIDE = 4
 DEPTH = 8
 HEAD = 128
 STEPS = (1, -1, 2)
+SECONDS = (2, 1, -1, 0)
+PIECES = 2
 
 
 def layer_norm(values):
@@ -59,33 +61,51 @@
 
 
 class Gather:
-    def __init__(self, place, buf, sems, send, pieces):
+    def __init__(self, place, buf, sems, send, pieces, relays=False):
         self.place, self.buf, self.sems, self.send, self.pieces = place, buf, sems, send, pieces
+        self.relays = relays
 
     def cols(self, piece):
         return pl.ds(piece * (HALF // self.pieces), HALF // self.pieces)
 
-    def pass_on(self, piece, half, slot, axis, base):
+    def pass_on(self, piece, half, slot, axis, base, steps):
         ref = self.buf.at[half, slot, :, self.cols(piece)]
-        for index, step in enumerate(STEPS):
+        for index, step in steps:
             push(ref, ref, self.send, self.sems.at[piece, half, base + index], self.place.along(axis, step))
 
+    def second(self, piece, half, slot):
+        steps = list(enumerate(STEPS))
+        self.pass_on(piece, half, slot, 1 - half, 3, steps[:2] if self.relays else steps)
+
     def start(self, piece):
-        for base in (0, 3):
-            for half in (0, 1):
-                own = self.place.slot(half, 0, 0)
-                self.pass_on(piece, half, own, half if base == 0 else 1 - half, base)
+        for half in (0, 1):
+            self.pass_on(piece, half, self.place.slot(half, 0, 0), half, 0, list(enumerate(STEPS)))
+        for half in (0, 1):
+            self.second(piece, half, self.place.slot(half, 0, 0))
 
     def forward(self, piece):
         for index, step in enumerate(STEPS):
             for half in (0, 1):
                 slot = self.place.slot(half, -step, 0)
                 await_bytes(self.buf.at[half, slot, :, self.cols(piece)], self.sems.at[piece, half, index])
-                self.pass_on(piece, half, slot, 1 - half, 3)
+                self.second(piece, half, slot)
+
+    def await_source(self, piece, half, index):
+        await_bytes(self.buf.at[half, pl.ds(0, 4), :, self.cols(piece)], self.sems.at[piece, half, 3 + index])
+
+    def relay(self, piece):
+        for index, firsts in enumerate(((0, 1), (2, 3))):
+            step = STEPS[index]
+            for half in (0, 1):
+                self.await_source(piece, half, index)
+                for first in firsts:
+                    slot = self.place.slot(half, first, -step)
+                    ref = self.buf.at[half, slot, :, self.cols(piece)]
+                    push(ref, ref, self.send, self.sems.at[piece, half, 5], self.place.along(1 - half, step))
 
     def finish(self, piece, half):
-        for index in range(3):
-            await_bytes(self.buf.at[half, pl.ds(0, 4), :, self.cols(piece)], self.sems.at[piece, half, 3 + index])
+        for index in range(2 if self.relays else 0, 3):
+            self.await_source(piece, half, index)
 
     def close(self):
         await_bytes(self.buf.at[:, pl.ds(0, 15)], self.send)
@@ -103,8 +123,9 @@
         a, b = (self.place.x, self.place.y) if half == 0 else (self.place.y, self.place.x)
         return lax.rem(a + first + SIDE, SIDE), lax.rem(b + second + SIDE, SIDE)
 
-    def start(self, piece):
-        for order, second in enumerate((2, 1, -1, 0)):
+    def start(self, piece, orders):
+        for order in orders:
+            second = SECONDS[order]
             for half in (0, 1):
                 for index, step in enumerate(STEPS):
                     one, two = self.at(half, step, second)
@@ -116,9 +137,10 @@
                         self.place.along(half, step),
                     )
 
-    def sums(self, piece):
+    def sums(self, piece, orders):
         cols = self.cols(piece)
-        for order, second in enumerate((2, 1, -1, 0)):
+        for order in orders:
+            second = SECONDS[order]
             for half in (0, 1):
                 await_bytes(self.landed.at[half, :, order, :, cols], self.sems.at[piece, half, order])
                 one, two = self.at(half, 0, second)
@@ -151,52 +173,43 @@
 
 
 class Handoff:
-    def __init__(self, place, buf, sems, sibling_sem, send, pieces):
-        self.place, self.buf, self.sems, self.sibling_sem = place, buf, sems, sibling_sem
-        self.send, self.pieces = send, pieces
+    def __init__(self, place, buf, sems, sibling_sems, send):
+        self.place, self.buf, self.sems, self.sibling_sems, self.send = place, buf, sems, sibling_sems, send
 
     def slot(self, step):
         return lax.rem(self.place.z + step + DEPTH, DEPTH) * 2 + self.place.core
 
-    def piece(self, slot, piece):
-        return self.buf.at[slot, :, pl.ds(piece * (WIDTH // self.pieces), WIDTH // self.pieces)]
-
     def carries(self, number, piece, side):
-        return number < 4 or (piece >= self.pieces // 2) == (side == 1)
+        return number < 4 or piece == side
 
     def onward(self, number, piece, side):
         way = (1, -1)[side]
-        ref = self.piece(self.slot(-way * number), piece)
+        ref = self.buf.at[piece, self.slot(-way * number)]
         push(ref, ref, self.send, self.sems.at[number, piece, side], self.place.up(way))
 
-    def across(self, slot):
-        ref = self.buf.at[slot]
-        push(ref, ref, self.send, self.sibling_sem, self.place.sibling())
+    def across(self, piece, slot):
+        ref = self.buf.at[piece, slot]
+        push(ref, ref, self.send, self.sibling_sems.at[piece], self.place.sibling())
 
     def start(self, piece):
         for side in (0, 1):
             self.onward(0, piece, side)
+        self.across(piece, self.slot(0))
 
     def step(self, number, piece):
         for side in (0, 1):
             if self.carries(number, piece, side):
                 slot = self.slot(-(1, -1)[side] * number)
-                await_bytes(self.piece(slot, piece), self.sems.at[number - 1, piece, side])
+                await_bytes(self.buf.at[piece, slot], self.sems.at[number - 1, piece, side])
                 if number < 4 and self.carries(number + 1, piece, side):
                     self.onward(number, piece, side)
-
-    def share(self, number):
-        if number == 0 or number == 4:
-            self.across(self.slot(number))
-        else:
-            self.across(self.slot(number))
-            self.across(self.slot(-number))
-
-    def finish(self):
-        await_bytes(self.buf.at[pl.ds(0, DEPTH)], self.sibling_sem)
+                self.across(piece, slot)
+
+    def finish(self, piece):
+        await_bytes(self.buf.at[piece, pl.ds(0, DEPTH)], self.sibling_sems.at[piece])
 
     def close(self):
-        await_bytes(self.buf.at[pl.ds(0, 15)], self.send)
+        await_bytes(self.buf.at[:, pl.ds(0, 15)], self.send)
 
 
 class Update:
@@ -264,18 +277,31 @@
     def second(self, half, step):
         return lax.rem((self.place.y if half == 0 else self.place.x) + step + SIDE, SIDE)
 
+    def share(self, half, step):
+        ref = self.buf.at[half, self.second(half, step), self.place.core]
+        push(ref, ref, self.send, self.sibling_sem, self.place.sibling())
+
     def start(self):
-        for step_index, step in enumerate(STEPS):
+        for index, step in enumerate((1, -1)):
             for half in (0, 1):
                 ref = self.buf.at[half, self.second(half, 0), self.place.core]
-                push(ref, ref, self.send, self.sems.at[half, step_index], self.place.along(1 - half, step))
-
-    def share(self):
-        for index, step in enumerate(STEPS):
+                push(ref, ref, self.send, self.sems.at[half, index], self.place.along(1 - half, step))
+
+    def relay(self):
+        for index, step in enumerate((1, -1)):
             for half in (0, 1):
                 ref = self.buf.at[half, self.second(half, -step), self.place.core]
                 await_bytes(ref, self.sems.at[half, index])
-                push(ref, ref, self.send, self.sibling_sem, self.place.sibling())
+                part = self.buf.at[half, self.second(half, -step), self.place.core, pl.ds(index * 32, 32)]
+                push(part, part, self.send, self.sems.at[half, 2 + index], self.place.along(1 - half, step))
+                self.share(half, -step)
+
+    def last(self):
+        for half in (0, 1):
+            for index in (0, 1):
+                part = self.buf.at[half, self.second(half, 2), self.place.core, pl.ds(index * 32, 32)]
+                await_bytes(part, self.sems.at[half, 2 + index])
+            self.share(half, 2)
 
     def finish(self):
         await_bytes(self.buf.at[0, pl.ds(0, 3)], self.sibling_sem)
@@ -322,7 +348,7 @@
     sc_sends,
     handed,
     hand_sems,
-    hand_sibling,
+    hand_siblings,
     hand_send,
     up_outgoing,
     up_incoming,
@@ -335,6 +361,7 @@
     text_in,
     text_kv,
     tscale,
+    text_stats,
 ):
     place = Place()
 
@@ -352,10 +379,53 @@
         loads.append(copy)
         return copy
 
+    def part_of(half, piece):
+        return pl.ds(half * HALF + piece * QUARTER, QUARTER)
+
     load_prompt = load(prompt_hbm, prompt)
-    load_ctx = load(ctx_hbm, ctx)
+    load_ctx = [
+        [load(ctx_hbm.at[:, part_of(half, piece)], ctx.at[:, part_of(half, piece)]) for half in (0, 1)]
+        for piece in range(PIECES)
+    ]
     load_latent = load(latent_hbm, latent)
     load_imod = load(imod_hbm, imod)
+
+    bounds, running = [], 0
+    for image in range(4):
+        running = running + lengths[0, image]
+        bounds.append(running)
+
+    def segments_of(row_ids):
+        return sum((row_ids >= bound).astype(jnp.int32) for bound in bounds)
+
+    rows_iota = lax.broadcasted_iota(jnp.int32, (16 * ROWS, 1), 0)
+    lanes_iota = lax.broadcasted_iota(jnp.int32, (1, 16 * ROWS), 1)
+    halves = (pl.ds(0, HALF), pl.ds(HALF, HALF))
+
+    load_prompt.wait()
+    row = lax.broadcasted_iota(jnp.int32, (256, 256), 0)
+    col = lax.broadcasted_iota(jnp.int32, (256, 256), 1)
+    ordered = []
+    for half in (0, 1):
+        block = row // 16
+        owner = block if half == 1 else lax.rem(block, 4) * 4 + block // 4
+        source = lax.rem(row // 4, 4) * 64 + owner * 4 + lax.rem(row, 4)
+        order = (col == source).astype(BF16)
+        ordered.append(jnp.dot(order, prompt[...], preferred_element_type=F32).astype(BF16))
+    text_scatter = Scatter(place, sc_buf, sc_landed, sc_mid, sc_own, sc_landed2, sc_sems, sc_sends, PIECES)
+    everything = range(len(SECONDS))
+
+    def embed(piece):
+        for half in (0, 1):
+            load_ctx[piece][half].wait()
+            product = jnp.dot(ordered[half], ctx[:, part_of(half, piece)], preferred_element_type=F32)
+            cols = text_scatter.cols(piece)
+            sc_buf[half, :, :, :, cols] = product.astype(BF16).reshape(4, 4, ROWS, QUARTER)
+
+    embed(0)
+    pl.semaphore_wait(barrier, len(partners))
+    text_scatter.start(0, everything)
+    embed(1)
     load_proj = [
         load(
             proj_hbm.at[pl.ds(share * 64, 64), pl.ds(half * HALF, HALF)],
@@ -368,39 +438,6 @@
     load_tmod = load(tmod_hbm, tmod)
     load_qkv = [load(qkv_hbm.at[part], qkv_w.at[:, pl.ds(part * HEAD, HEAD)]) for part in range(3)]
 
-    bounds, running = [], 0
-    for image in range(4):
-        running = running + lengths[0, image]
-        bounds.append(running)
-
-    def segments_of(row_ids):
-        return sum((row_ids >= bound).astype(jnp.int32) for bound in bounds)
-
-    rows_iota = lax.broadcasted_iota(jnp.int32, (16 * ROWS, 1), 0)
-    lanes_iota = lax.broadcasted_iota(jnp.int32, (1, 16 * ROWS), 1)
-    halves = (pl.ds(0, HALF), pl.ds(HALF, HALF))
-
-    load_prompt.wait()
-    row = lax.broadcasted_iota(jnp.int32, (256, 256), 0)
-    col = lax.broadcasted_iota(jnp.int32, (256, 256), 1)
-    ordered = []
-    for half in (0, 1):
-        block = row // 16
-        owner = block if half == 1 else lax.rem(block, 4) * 4 + block // 4
-        source = lax.rem(row // 4, 4) * 64 + owner * 4 + lax.rem(row, 4)
-        order = (col == source).astype(BF16)
-        ordered.append(jnp.dot(order, prompt[...], preferred_element_type=F32).astype(BF16))
-    load_ctx.wait()
-    for half in (0, 1):
-        for piece in range(3):
-            weight = ctx[:, pl.ds(half * HALF + piece * 512, 512)]
-            product = jnp.dot(ordered[half], weight, preferred_element_type=F32)
-            sc_buf[half, :, :, :, pl.ds(piece * 512, 512)] = product.astype(BF16).reshape(4, 4, ROWS, 512)
-
-    pl.semaphore_wait(barrier, len(partners))
-    text_scatter = Scatter(place, sc_buf, sc_landed, sc_mid, sc_own, sc_landed2, sc_sems, sc_sends, 1)
-    text_scatter.start(0)
-
     load_imod.wait()
     mine = segments_of(place.tp * ROWS + lax.broadcasted_iota(jnp.int32, (ROWS, 1), 0))
     for step in (0, 1):
@@ -420,27 +457,32 @@
         values = layer_norm(x_state[...])
         put_block(step, (values * rows_mod[step, 1] + rows_mod[step, 0]).astype(BF16))
 
-    def gather_of(which):
-        return Gather(place, gathered.at[which], gather_sems.at[which], gather_sends.at[which], 1)
+    def gather_of(which, pieces=1, relays=False):
+        return Gather(place, gathered.at[which], gather_sems.at[which], gather_sends.at[which], pieces, relays)
 
     put_image(0)
-    text_scatter.sums(0)
-    first_gather = gather_of(0)
+    for order in everything:
+        text_scatter.sums(0, (order,))
+        text_scatter.start(1, (order,))
+
+    handoff = Handoff(place, handed, hand_sems, hand_siblings, hand_send)
+
+    def hand_out(piece):
+        for half in (0, 1):
+            cols = pl.ds(half * QUARTER, QUARTER)
+            handed[piece, place.group, :, cols] = text_scatter.result(piece, half).astype(BF16)
+        handoff.start(piece)
+
+    text_scatter.sums(1, everything[:3])
+    hand_out(0)
+    text_scatter.sums(1, everything[3:])
+    first_gather = gather_of(0, relays=True)
     first_gather.start(0)
-
-    handoff = Handoff(place, handed, hand_sems, hand_sibling, hand_send, 2)
-    for half in (0, 1):
-        handed[place.group, :, halves[half]] = text_scatter.result(0, half).astype(BF16)
-        handoff.start(half)
-    handoff.share(0)
-
-    def hand_step(number):
-        for piece in (0, 1):
-            handoff.step(number, piece)
-        handoff.share(number)
-
+    hand_out(1)
+    handoff.step(1, 0)
     first_gather.forward(0)
-    hand_step(1)
+    handoff.step(1, 1)
+    handoff.step(2, 0)
     for copy in load_proj:
         copy.wait()
     weights = ProjectionWeights(place, proj_w, proj_sems, proj_sibling, proj_send)
@@ -457,10 +499,10 @@
         txt_w[at, HEAD:] = parted[128:]
         return carry
 
-    lax.fori_loop(0, 12, part_weights, 0)
-    hand_step(2)
-    lax.fori_loop(12, 24, part_weights, 0)
-    hand_step(3)
+    lax.fori_loop(0, 24, part_weights, 0)
+    handoff.step(2, 1)
+    handoff.step(3, 0)
+    first_gather.relay(0)
 
     load_tmod.wait()
     slot_image = lax.broadcasted_iota(jnp.int32, (ROWS, 1), 0) // 4
@@ -470,7 +512,9 @@
             for image in range(4):
                 rows = jnp.where(slot_image == image, tmod[image, step, kind : kind + 1, :], rows)
             tscale[step, kind] = rows + float(kind)
-    hand_step(4)
+    handoff.step(3, 1)
+    handoff.step(4, 0)
+    weights.relay()
 
     pick_row = lax.broadcasted_iota(jnp.int32, (ROWS, 256), 0)
     pick_col = lax.broadcasted_iota(jnp.int32, (ROWS, 256), 1)
@@ -478,21 +522,22 @@
     for image in range(4):
         wanted = jnp.where(pick_row // 4 == image, prompt_ids[place.group * 4 + image] * 4, wanted)
     pick = (pick_col == wanted + lax.rem(pick_row, 4)).astype(BF16)
-    handoff.finish()
-    slot_text = jnp.concatenate(
-        [
-            jnp.dot(
-                pick,
-                handed[:, :, pl.ds(piece * 512, 512)].reshape(256, 512),
-                preferred_element_type=F32,
-            )
-            for piece in range(6)
-        ],
-        axis=1,
-    )
-    put_block(2, layer_norm(slot_text).astype(BF16))
-    text_gather = gather_of(2)
-    text_gather.start(0)
+    text_gather = gather_of(2, PIECES)
+
+    def take_text(piece):
+        handoff.finish(piece)
+        for half in (0, 1):
+            held = handed[piece, :, :, pl.ds(half * QUARTER, QUARTER)].reshape(256, QUARTER)
+            taken = jnp.dot(pick, held, preferred_element_type=F32).astype(BF16)
+            gathered[2, half, place.tp, :, text_gather.cols(piece)] = taken
+        text_gather.start(piece)
+
+    take_text(0)
+    handoff.step(4, 1)
+    take_text(1)
+    text_gather.forward(0)
+    weights.last()
+    text_gather.forward(1)
 
     def project_image(which, gather):
         total = None
@@ -512,7 +557,8 @@
         for half in (0, 1):
 
             def modulate(owner, carry):
-                normed = gathered[2, half, owner].astype(F32)
+                center, scale = text_stats[0, owner], text_stats[1, owner]
+                normed = (gathered[2, half, owner].astype(F32) - center[:, :1]) * scale[:, :1]
                 scaled = normed * tscale[step, 1, :, halves[half]] + tscale[step, 0, :, halves[half]]
                 text_in[half, owner] = scaled.astype(BF16)
                 return carry
@@ -555,14 +601,24 @@
             state = x_state[:, halves[half]] + gate * update.result(half)
             x_state[:, halves[half]] = state.astype(BF16).astype(F32)
 
-    weights.share()
-    text_gather.forward(0)
     for copy in load_qkv:
         copy.wait()
     queries, keys, values = project_image(0, first_gather)
     weights.finish()
-    for half in (0, 1):
-        text_gather.finish(0, half)
+
+    means, squares = [], []
+    for piece in range(PIECES):
+        parts = []
+        for half in (0, 1):
+            text_gather.finish(piece, half)
+            parts.append(gathered[2, half, :, :, text_gather.cols(piece)].reshape(256, QUARTER).astype(F32))
+        mean = sum(jnp.sum(part, -1, keepdims=True) for part in parts) / HALF
+        means.append(mean)
+        squares.append(sum(jnp.sum((part - mean) * (part - mean), -1, keepdims=True) for part in parts))
+    gap = (means[0] - means[1]) * 0.5
+    deviation = lax.rsqrt((squares[0] + squares[1]) / WIDTH + gap * gap + 1e-6)
+    text_stats[0] = jnp.broadcast_to((means[0] + means[1]) * 0.5, (256, HEAD)).reshape(16, ROWS, HEAD)
+    text_stats[1] = jnp.broadcast_to(deviation, (256, HEAD)).reshape(16, ROWS, HEAD)
     project_text(0)
 
     first_update = update_of(0)
@@ -619,23 +675,23 @@
             pltpu.VMEM((2 * WIDTH, HEAD), BF16),
             pltpu.VMEM((WIDTH, 2 * HEAD), BF16),
             pltpu.VMEM((2, 4, 2, 64, HALF), BF16),
-            dma((13,)),
-            dma((2, 3)),
+            dma((16,)),
+            dma((2, 4)),
             dma,
             dma,
             pltpu.VMEM((3, 2, 16) + block, BF16),
-            dma((3, 1, 2, 6)),
+            dma((3, PIECES, 2, 6)),
             dma((3,)),
             pltpu.VMEM((2, 4, 4) + block, BF16),
             pltpu.VMEM((2, 3, 4) + block, BF16),
             pltpu.VMEM((2, 3) + block, BF16),
             pltpu.VMEM((2,) + block, F32),
             pltpu.VMEM((2, 3) + block, BF16),
-            dma((1, 2, 5)),
+            dma((PIECES, 2, 5)),
             dma((2,)),
-            pltpu.VMEM((16, ROWS, WIDTH), BF16),
-            dma((4, 2, 2)),
-            dma,
+            pltpu.VMEM((PIECES, 16) + block, BF16),
+            dma((4, PIECES, 2)),
+            dma((PIECES,)),
             dma,
             pltpu.VMEM((2, 2, 4, 4, ROWS, HEAD), BF16),
             pltpu.VMEM((2, 2, 4, 4, ROWS, HEAD), BF16),
@@ -648,6 +704,7 @@
             pltpu.VMEM((2, 16) + block, BF16),
             pltpu.VMEM((256, 2 * HEAD), BF16),
             pltpu.VMEM((2, 2, ROWS, WIDTH), F32),
+            pltpu.VMEM((2, 16, ROWS, HEAD), F32),
         ],
         compiler_params=pltpu.CompilerParams(
             collective_id=0, has_side_effects=True, vmem_limit_bytes=56 * 1024 * 1024

time: 89.3 us -> 92.2 us (1.032)
  Pallas kernels: 87.6 us -> 90.2 us
    pallas_call x1, Pallas kernels: 87.6 us -> 90.2 us  [on_device(): pl.pallas_call(kernel, out_shape=jax.ShapeDtypeStruct((ROWS, WIDTH), BF16...]
where the time goes in v3:
time: 92.2 us; the launch traced here: 91.8 us
  Pallas kernels  90.2 us (98%)
  local copies, waits for them, and re-layouts  1.54 us (2%)
    pallas_call x1, Pallas kernels, on_device(): pl.pallas_call(kernel, out_shape=jax.ShapeDtypeStruct((ROWS, WIDTH), BF16...  90.2 us

profile of v3, /device:TPU:32, one launch (start us, length us, event | category | flops | bytes accessed | tf_op | source)
XLA Modules:
  0.0 91.8 jit_solution(10643767883213702366)
XLA Ops:
  0.0 90.2 %shard_map.109 = bf16[16,3072]{1,0:T(8,128)(2,1)} custom-call(s32[64]{0:T(128)} %prompt_ids.1, s32[1,4]{1,0:T(1,128)} %lengths.1, bf16[256,256]{1,0:T(8,128)(2,1)} %bitcast.14, bf16[256,3072]{1,0:T(8,128)(2,1)} %ctx_hbm.1, bf16[16,3072]{1,0:T(8,128)(2,1)} %bitcast.15, f32[4,3,2,3072]{3,2,1,0:T(2,128)} %bitcast.12, f32[4,2,2,3072]{3,2,1,0:T(2,128)} %bitcast.13, ...), custom_call_target="tpu_custom_call" | custom-call | tf_op jit(solution)/shard_map/pallas_call | solution.py:663
  90.2 1.5 %copy.13 = bf16[1,16,3072]{2,1,0:T(8,128)(2,1)} copy(bf16[1,16,3072]{2,1,0:T(8,128)(2,1)} %bitcast.11) | data formatting | bytes 196608

commit v4 on v3

--- a/solution.py
+++ b/solution.py
@@ -9,14 +9,12 @@
 
 MESH = pl.DeviceIdType.MESH
 F32, BF16 = jnp.float32, jnp.bfloat16
-WIDTH, HALF, QUARTER = 3072, 1536, 768
+WIDTH, HALF = 3072, 1536
 ROWS = 16
 SIDE = 4
 DEPTH = 8
 HEAD = 128
 STEPS = (1, -1, 2)
-SECONDS = (2, 1, -1, 0)
-PIECES = 2
 
 
 def layer_norm(values):
@@ -61,114 +59,117 @@
 
 
 class Gather:
-    def __init__(self, place, buf, sems, send, pieces, relays=False):
-        self.place, self.buf, self.sems, self.send, self.pieces = place, buf, sems, send, pieces
-        self.relays = relays
-
-    def cols(self, piece):
-        return pl.ds(piece * (HALF // self.pieces), HALF // self.pieces)
-
-    def pass_on(self, piece, half, slot, axis, base, steps):
-        ref = self.buf.at[half, slot, :, self.cols(piece)]
-        for index, step in steps:
-            push(ref, ref, self.send, self.sems.at[piece, half, base + index], self.place.along(axis, step))
-
-    def second(self, piece, half, slot):
-        steps = list(enumerate(STEPS))
-        self.pass_on(piece, half, slot, 1 - half, 3, steps[:2] if self.relays else steps)
-
-    def start(self, piece):
-        for half in (0, 1):
-            self.pass_on(piece, half, self.place.slot(half, 0, 0), half, 0, list(enumerate(STEPS)))
-        for half in (0, 1):
-            self.second(piece, half, self.place.slot(half, 0, 0))
-
-    def forward(self, piece):
-        for index, step in enumerate(STEPS):
+    def __init__(self, place, buf, sems, send):
+        self.place, self.buf, self.sems, self.send = place, buf, sems, send
+
+    def pass_on(self, half, first, second, axis, step, sem):
+        ref = self.buf.at[half, self.place.slot(half, first, second)]
+        push(ref, ref, self.send, self.sems.at[half, sem], self.place.along(axis, step))
+
+    def start(self):
+        for index in (2, 0, 1):
             for half in (0, 1):
-                slot = self.place.slot(half, -step, 0)
-                await_bytes(self.buf.at[half, slot, :, self.cols(piece)], self.sems.at[piece, half, index])
-                self.second(piece, half, slot)
-
-    def await_source(self, piece, half, index):
-        await_bytes(self.buf.at[half, pl.ds(0, 4), :, self.cols(piece)], self.sems.at[piece, half, 3 + index])
-
-    def relay(self, piece):
-        for index, firsts in enumerate(((0, 1), (2, 3))):
+                self.pass_on(half, 0, 0, half, STEPS[index], index)
+            if index == 2:
+                for half in (0, 1):
+                    self.pass_on(half, 0, 0, 1 - half, 2, 5)
+        for index in (0, 1):
+            for half in (0, 1):
+                self.pass_on(half, 0, 0, 1 - half, STEPS[index], 3 + index)
+
+    def forward(self):
+        for index in (0, 1, 2):
             step = STEPS[index]
             for half in (0, 1):
-                self.await_source(piece, half, index)
-                for first in firsts:
-                    slot = self.place.slot(half, first, -step)
-                    ref = self.buf.at[half, slot, :, self.cols(piece)]
-                    push(ref, ref, self.send, self.sems.at[piece, half, 5], self.place.along(1 - half, step))
-
-    def finish(self, piece, half):
-        for index in range(2 if self.relays else 0, 3):
-            self.await_source(piece, half, index)
+                await_bytes(self.buf.at[half, self.place.slot(half, -step, 0)], self.sems.at[half, index])
+                for other in (0, 1):
+                    self.pass_on(half, -step, 0, 1 - half, STEPS[other], 6 + other)
+            if index == 1:
+                for half in (0, 1):
+                    await_bytes(self.buf.at[half, self.place.slot(half, 0, 2)], self.sems.at[half, 5])
+                    for onward in (2, 1, -1):
+                        self.pass_on(half, 0, 2, half, onward, 8)
+
+    def finish(self, half):
+        for index in (0, 1):
+            await_bytes(self.buf.at[half, self.place.slot(half, 0, -STEPS[index])], self.sems.at[half, 3 + index])
+        for index in (6, 7, 8):
+            await_bytes(self.buf.at[half, pl.ds(0, 3)], self.sems.at[half, index])
 
     def close(self):
         await_bytes(self.buf.at[:, pl.ds(0, 15)], self.send)
 
 
 class Scatter:
-    def __init__(self, place, buf, landed, mid, own, landed2, sems, send, pieces):
-        self.place, self.buf, self.landed, self.mid = place, buf, landed, mid
-        self.own, self.landed2, self.sems, self.send, self.pieces = own, landed2, sems, send, pieces
-
-    def cols(self, piece):
-        return pl.ds(piece * (HALF // self.pieces), HALF // self.pieces)
-
-    def at(self, half, first, second):
+    def __init__(self, place, buf, sides, line, mid, landed, sems, send, sent):
+        self.place, self.buf, self.sides, self.line = place, buf, sides, line
+        self.mid, self.landed, self.sems, self.send, self.sent = mid, landed, sems, send, sent
+
+    def block(self, half, first, second):
         a, b = (self.place.x, self.place.y) if half == 0 else (self.place.y, self.place.x)
-        return lax.rem(a + first + SIDE, SIDE), lax.rem(b + second + SIDE, SIDE)
-
-    def start(self, piece, orders):
-        for order in orders:
-            second = SECONDS[order]
+        return self.buf.at[half, lax.rem(a + first + SIDE, SIDE), lax.rem(b + second + SIDE, SIDE)]
+
+    def start(self):
+        for index in (2, 0, 1):
             for half in (0, 1):
-                for index, step in enumerate(STEPS):
-                    one, two = self.at(half, step, second)
+                push(
+                    self.block(half, STEPS[index], 2),
+                    self.line.at[half, index],
+                    self.send.at[0],
+                    self.sems.at[half, 3],
+                    self.place.along(half, STEPS[index]),
+                )
+            for half in (0, 1):
+                for side in (0, 1):
                     push(
-                        self.buf.at[half, one, two, :, self.cols(piece)],
-                        self.landed.at[half, index, order, :, self.cols(piece)],
+                        self.block(half, STEPS[index], STEPS[side]),
+                        self.sides.at[half, index, side],
                         self.send.at[0],
-                        self.sems.at[piece, half, order],
-                        self.place.along(half, step),
+                        self.sems.at[half, index],
+                        self.place.along(1 - half, STEPS[side]),
                     )
-
-    def sums(self, piece, orders):
-        cols = self.cols(piece)
-        for order in orders:
-            second = SECONDS[order]
+        for half in (0, 1):
+            for side in (0, 1):
+                push(
+                    self.block(half, 0, STEPS[side]),
+                    self.landed.at[half, 3 + side],
+                    self.send.at[0],
+                    self.sems.at[half, 4],
+                    self.place.along(1 - half, STEPS[side]),
+                )
+
+    def sums(self):
+        for index in (2, 3, 0, 1):
             for half in (0, 1):
-                await_bytes(self.landed.at[half, :, order, :, cols], self.sems.at[piece, half, order])
-                one, two = self.at(half, 0, second)
-                total = self.buf[half, one, two, :, cols].astype(F32)
-                for index in range(3):
-                    total = total + self.landed[half, index, order, :, cols].astype(F32)
-                if second == 0:
-                    self.own[half, :, cols] = total
+                if index < 3:
+                    landed, own, axis, step = self.sides.at[half, index], (STEPS[index], 0), half, STEPS[index]
+                    count, goal = 2, index
                 else:
-                    self.mid[half, order, :, cols] = total.astype(BF16)
-                    push(
-                        self.mid.at[half, order, :, cols],
-                        self.landed2.at[half, order, :, cols],
-                        self.send.at[1],
-                        self.sems.at[piece, half, 4],
-                        self.place.along(1 - half, second),
-                    )
-
-    def result(self, piece, half):
-        cols = self.cols(piece)
-        await_bytes(self.landed2.at[half, :, :, cols], self.sems.at[piece, half, 4])
-        total = self.own[half, :, cols]
-        for index in range(3):
-            total = total + self.landed2[half, index, :, cols].astype(F32)
+                    landed, own, axis, step = self.line.at[half], (0, 2), 1 - half, 2
+                    count, goal = 3, 5
+                await_bytes(landed, self.sems.at[half, index])
+                total = self.block(half, *own)[...].astype(F32)
+                for other in range(count):
+                    total = total + landed[other].astype(F32)
+                self.mid[half, index] = total.astype(BF16)
+                push(
+                    self.mid.at[half, index],
+                    self.landed.at[half, goal],
+                    self.send.at[1],
+                    self.sems.at[half, 5],
+                    self.place.along(axis, step),
+                )
+
+    def result(self, half):
+        await_bytes(self.landed.at[half, pl.ds(0, 2)], self.sems.at[half, 4])
+        await_bytes(self.landed.at[half, pl.ds(0, 4)], self.sems.at[half, 5])
+        total = self.block(half, 0, 0)[...].astype(F32)
+        for other in range(6):
+            total = total + self.landed[half, other].astype(F32)
         return total
 
     def close(self):
-        await_bytes(self.buf.at[:, pl.ds(0, 3)], self.send.at[0])
+        await_bytes(self.sent, self.send.at[0])
         await_bytes(self.mid, self.send.at[1])
 
 
@@ -179,31 +180,42 @@
     def slot(self, step):
         return lax.rem(self.place.z + step + DEPTH, DEPTH) * 2 + self.place.core
 
-    def carries(self, number, piece, side):
-        return number < 4 or piece == side
-
-    def onward(self, number, piece, side):
+    def onward(self, piece, side, held, goal):
         way = (1, -1)[side]
-        ref = self.buf.at[piece, self.slot(-way * number)]
-        push(ref, ref, self.send, self.sems.at[number, piece, side], self.place.up(way))
+        ref = self.buf.at[piece, self.slot(-way * held)]
+        push(ref, ref, self.send, self.sems.at[piece, side, goal - 1], self.place.up(way * (goal - held)))
 
     def across(self, piece, slot):
         ref = self.buf.at[piece, slot]
         push(ref, ref, self.send, self.sibling_sems.at[piece], self.place.sibling())
 
+    def take(self, piece, side, number):
+        slot = self.slot(-(1, -1)[side] * number)
+        await_bytes(self.buf.at[piece, slot], self.sems.at[piece, side, number - 1])
+        return slot
+
     def start(self, piece):
+        for goal in (2, 1):
+            for side in (0, 1):
+                self.onward(piece, side, 0, goal)
+        self.across(piece, self.slot(0))
+
+    def pass_on(self, piece):
         for side in (0, 1):
-            self.onward(0, piece, side)
-        self.across(piece, self.slot(0))
-
-    def step(self, number, piece):
+            slot = self.take(piece, side, 2)
+            if piece == side:
+                self.onward(piece, side, 2, 4)
+            self.onward(piece, side, 2, 3)
+            self.across(piece, slot)
+
+    def near(self, piece):
         for side in (0, 1):
-            if self.carries(number, piece, side):
-                slot = self.slot(-(1, -1)[side] * number)
-                await_bytes(self.buf.at[piece, slot], self.sems.at[number - 1, piece, side])
-                if number < 4 and self.carries(number + 1, piece, side):
-                    self.onward(number, piece, side)
-                self.across(piece, slot)
+            self.across(piece, self.take(piece, side, 1))
+
+    def far(self, piece):
+        for side in (0, 1):
+            self.across(piece, self.take(piece, side, 3))
+        self.across(piece, self.take(piece, piece, 4))
 
     def finish(self, piece):
         await_bytes(self.buf.at[piece, pl.ds(0, DEPTH)], self.sibling_sems.at[piece])
@@ -340,10 +352,10 @@
     gather_sems,
     gather_sends,
     sc_buf,
+    sc_sides,
+    sc_line,
+    sc_mid,
     sc_landed,
-    sc_mid,
-    sc_own,
-    sc_landed2,
     sc_sems,
     sc_sends,
     handed,
@@ -361,13 +373,12 @@
     text_in,
     text_kv,
     tscale,
-    text_stats,
 ):
     place = Place()
 
     barrier = pltpu.get_barrier_semaphore()
     partners = [place.along(axis, step) for axis in (0, 1) for step in STEPS]
-    partners += [place.up(1), place.up(-1), place.sibling()]
+    partners += [place.up(1), place.up(-1), place.up(2), place.up(-2), place.sibling()]
     for partner in partners:
         pl.semaphore_signal(barrier, inc=1, device_id=partner, device_id_type=MESH)
 
@@ -379,14 +390,9 @@
         loads.append(copy)
         return copy
 
-    def part_of(half, piece):
-        return pl.ds(half * HALF + piece * QUARTER, QUARTER)
-
+    halves = (pl.ds(0, HALF), pl.ds(HALF, HALF))
     load_prompt = load(prompt_hbm, prompt)
-    load_ctx = [
-        [load(ctx_hbm.at[:, part_of(half, piece)], ctx.at[:, part_of(half, piece)]) for half in (0, 1)]
-        for piece in range(PIECES)
-    ]
+    load_ctx = [load(ctx_hbm.at[:, cols], ctx.at[:, cols]) for cols in halves]
     load_latent = load(latent_hbm, latent)
     load_imod = load(imod_hbm, imod)
 
@@ -400,7 +406,6 @@
 
     rows_iota = lax.broadcasted_iota(jnp.int32, (16 * ROWS, 1), 0)
     lanes_iota = lax.broadcasted_iota(jnp.int32, (1, 16 * ROWS), 1)
-    halves = (pl.ds(0, HALF), pl.ds(HALF, HALF))
 
     load_prompt.wait()
     row = lax.broadcasted_iota(jnp.int32, (256, 256), 0)
@@ -412,20 +417,17 @@
         source = lax.rem(row // 4, 4) * 64 + owner * 4 + lax.rem(row, 4)
         order = (col == source).astype(BF16)
         ordered.append(jnp.dot(order, prompt[...], preferred_element_type=F32).astype(BF16))
-    text_scatter = Scatter(place, sc_buf, sc_landed, sc_mid, sc_own, sc_landed2, sc_sems, sc_sends, PIECES)
-    everything = range(len(SECONDS))
-
-    def embed(piece):
-        for half in (0, 1):
-            load_ctx[piece][half].wait()
-            product = jnp.dot(ordered[half], ctx[:, part_of(half, piece)], preferred_element_type=F32)
-            cols = text_scatter.cols(piece)
-            sc_buf[half, :, :, :, cols] = product.astype(BF16).reshape(4, 4, ROWS, QUARTER)
-
-    embed(0)
+    for half in (0, 1):
+        load_ctx[half].wait()
+        for piece in range(3):
+            product = jnp.dot(ordered[half], ctx[:, pl.ds(half * HALF + piece * 512, 512)], preferred_element_type=F32)
+            sc_buf[half, :, :, :, pl.ds(piece * 512, 512)] = product.astype(BF16).reshape(4, 4, ROWS, 512)
+
     pl.semaphore_wait(barrier, len(partners))
-    text_scatter.start(0, everything)
-    embed(1)
+    text_scatter = Scatter(
+        place, sc_buf, sc_sides, sc_line, sc_mid, sc_landed, sc_sems, sc_sends, gathered.at[1, :, pl.ds(0, 11)]
+    )
+    text_scatter.start()
     load_proj = [
         load(
             proj_hbm.at[pl.ds(share * 64, 64), pl.ds(half * HALF, HALF)],
@@ -457,36 +459,28 @@
         values = layer_norm(x_state[...])
         put_block(step, (values * rows_mod[step, 1] + rows_mod[step, 0]).astype(BF16))
 
-    def gather_of(which, pieces=1, relays=False):
-        return Gather(place, gathered.at[which], gather_sems.at[which], gather_sends.at[which], pieces, relays)
+    def gather_of(which):
+        return Gather(place, gathered.at[which], gather_sems.at[which], gather_sends.at[which])
 
     put_image(0)
-    for order in everything:
-        text_scatter.sums(0, (order,))
-        text_scatter.start(1, (order,))
+    text_scatter.sums()
+    first_gather = gather_of(0)
+    first_gather.start()
 
     handoff = Handoff(place, handed, hand_sems, hand_siblings, hand_send)
-
-    def hand_out(piece):
-        for half in (0, 1):
-            cols = pl.ds(half * QUARTER, QUARTER)
-            handed[piece, place.group, :, cols] = text_scatter.result(piece, half).astype(BF16)
-        handoff.start(piece)
-
-    text_scatter.sums(1, everything[:3])
-    hand_out(0)
-    text_scatter.sums(1, everything[3:])
-    first_gather = gather_of(0, relays=True)
-    first_gather.start(0)
-    hand_out(1)
-    handoff.step(1, 0)
-    first_gather.forward(0)
-    handoff.step(1, 1)
-    handoff.step(2, 0)
+    for half in (0, 1):
+        handed[half, place.group] = text_scatter.result(half).astype(BF16)
+        handoff.start(half)
+    first_gather.forward()
+    for half in (0, 1):
+        handoff.pass_on(half)
     for copy in load_proj:
         copy.wait()
     weights = ProjectionWeights(place, proj_w, proj_sems, proj_sibling, proj_send)
     weights.start()
+
+    for half in (0, 1):
+        handoff.near(half)
 
     load_txt.wait()
     unweave = (col == lax.rem(row, 128) * 2 + row // 128).astype(BF16)
@@ -500,10 +494,6 @@
         return carry
 
     lax.fori_loop(0, 24, part_weights, 0)
-    handoff.step(2, 1)
-    handoff.step(3, 0)
-    first_gather.relay(0)
-
     load_tmod.wait()
     slot_image = lax.broadcasted_iota(jnp.int32, (ROWS, 1), 0) // 4
     for step in (0, 1):
@@ -512,9 +502,6 @@
             for image in range(4):
                 rows = jnp.where(slot_image == image, tmod[image, step, kind : kind + 1, :], rows)
             tscale[step, kind] = rows + float(kind)
-    handoff.step(3, 1)
-    handoff.step(4, 0)
-    weights.relay()
 
     pick_row = lax.broadcasted_iota(jnp.int32, (ROWS, 256), 0)
     pick_col = lax.broadcasted_iota(jnp.int32, (ROWS, 256), 1)
@@ -522,27 +509,24 @@
     for image in range(4):
         wanted = jnp.where(pick_row // 4 == image, prompt_ids[place.group * 4 + image] * 4, wanted)
     pick = (pick_col == wanted + lax.rem(pick_row, 4)).astype(BF16)
-    text_gather = gather_of(2, PIECES)
-
-    def take_text(piece):
-        handoff.finish(piece)
-        for half in (0, 1):
-            held = handed[piece, :, :, pl.ds(half * QUARTER, QUARTER)].reshape(256, QUARTER)
-            taken = jnp.dot(pick, held, preferred_element_type=F32).astype(BF16)
-            gathered[2, half, place.tp, :, text_gather.cols(piece)] = taken
-        text_gather.start(piece)
-
-    take_text(0)
-    handoff.step(4, 1)
-    take_text(1)
-    text_gather.forward(0)
-    weights.last()
-    text_gather.forward(1)
+    for half in (0, 1):
+        handoff.far(half)
+    taken = []
+    for half in (0, 1):
+        handoff.finish(half)
+        for piece in range(3):
+            held = handed[half, :, :, pl.ds(piece * 512, 512)].reshape(256, 512)
+            taken.append(jnp.dot(pick, held, preferred_element_type=F32))
+    put_block(2, layer_norm(jnp.concatenate(taken, axis=1)).astype(BF16))
+    text_gather = gather_of(2)
+    text_gather.start()
+    weights.relay()
+    text_gather.forward()
 
     def project_image(which, gather):
         total = None
         for half in (0, 1):
-            gather.finish(0, half)
+            gather.finish(half)
             term = jnp.dot(
                 gathered[which, half].reshape(256, HALF),
                 qkv_w[pl.ds(half * HALF, HALF), :],
@@ -557,8 +541,7 @@
         for half in (0, 1):
 
             def modulate(owner, carry):
-                center, scale = text_stats[0, owner], text_stats[1, owner]
-                normed = (gathered[2, half, owner].astype(F32) - center[:, :1]) * scale[:, :1]
+                normed = gathered[2, half, owner].astype(F32)
                 scaled = normed * tscale[step, 1, :, halves[half]] + tscale[step, 0, :, halves[half]]
                 text_in[half, owner] = scaled.astype(BF16)
                 return carry
@@ -604,33 +587,22 @@
     for copy in load_qkv:
         copy.wait()
     queries, keys, values = project_image(0, first_gather)
-    weights.finish()
-
-    means, squares = [], []
-    for piece in range(PIECES):
-        parts = []
-        for half in (0, 1):
-            text_gather.finish(piece, half)
-            parts.append(gathered[2, half, :, :, text_gather.cols(piece)].reshape(256, QUARTER).astype(F32))
-        mean = sum(jnp.sum(part, -1, keepdims=True) for part in parts) / HALF
-        means.append(mean)
-        squares.append(sum(jnp.sum((part - mean) * (part - mean), -1, keepdims=True) for part in parts))
-    gap = (means[0] - means[1]) * 0.5
-    deviation = lax.rsqrt((squares[0] + squares[1]) / WIDTH + gap * gap + 1e-6)
-    text_stats[0] = jnp.broadcast_to((means[0] + means[1]) * 0.5, (256, HEAD)).reshape(16, ROWS, HEAD)
-    text_stats[1] = jnp.broadcast_to(deviation, (256, HEAD)).reshape(16, ROWS, HEAD)
+    weights.last()
+    for half in (0, 1):
+        text_gather.finish(half)
     project_text(0)
 
     first_update = update_of(0)
     first_update.start(attend(queries, keys, values))
+    weights.finish()
     first_update.multiply()
     project_text(1)
     advance(0, first_update)
 
     put_image(1)
     second_gather = gather_of(1)
-    second_gather.start(0)
-    second_gather.forward(0)
+    second_gather.start()
+    second_gather.forward()
     queries, keys, values = project_image(1, second_gather)
     second_update = update_of(1)
     second_update.start(attend(queries, keys, values))
@@ -675,23 +647,23 @@
             pltpu.VMEM((2 * WIDTH, HEAD), BF16),
             pltpu.VMEM((WIDTH, 2 * HEAD), BF16),
             pltpu.VMEM((2, 4, 2, 64, HALF), BF16),
-            dma((16,)),
+            dma((14,)),
             dma((2, 4)),
             dma,
             dma,
             pltpu.VMEM((3, 2, 16) + block, BF16),
-            dma((3, PIECES, 2, 6)),
+            dma((3, 2, 9)),
             dma((3,)),
             pltpu.VMEM((2, 4, 4) + block, BF16),
-            pltpu.VMEM((2, 3, 4) + block, BF16),
+            pltpu.VMEM((2, 3, 2) + block, BF16),
             pltpu.VMEM((2, 3) + block, BF16),
-            pltpu.VMEM((2,) + block, F32),
-            pltpu.VMEM((2, 3) + block, BF16),
-            dma((PIECES, 2, 5)),
+            pltpu.VMEM((2, 4) + block, BF16),
+            pltpu.VMEM((2, 6) + block, BF16),
+            dma((2, 6)),
             dma((2,)),
-            pltpu.VMEM((PIECES, 16) + block, BF16),
-            dma((4, PIECES, 2)),
-            dma((PIECES,)),
+            pltpu.VMEM((2, 16) + block, BF16),
+            dma((2, 2, 4)),
+            dma((2,)),
             dma,
             pltpu.VMEM((2, 2, 4, 4, ROWS, HEAD), BF16),
             pltpu.VMEM((2, 2, 4, 4, ROWS, HEAD), BF16),
@@ -704,7 +676,6 @@
             pltpu.VMEM((2, 16) + block, BF16),
             pltpu.VMEM((256, 2 * HEAD), BF16),
             pltpu.VMEM((2, 2, ROWS, WIDTH), F32),
-            pltpu.VMEM((2, 16, ROWS, HEAD), F32),
         ],
         compiler_params=pltpu.CompilerParams(
             collective_id=0, has_side_effects=True, vmem_limit_bytes=56 * 1024 * 1024

time: 92.2 us -> 87 us (0.944)
  Pallas kernels: 90.2 us -> 85.3 us
    pallas_call x1, Pallas kernels: 90.2 us -> 85.3 us  [on_device(): pl.pallas_call(kernel, out_shape=jax.ShapeDtypeStruct((ROWS, WIDTH), BF16...]
where the time goes in v4:
time: 87 us; the launch traced here: 86.8 us
  Pallas kernels  85.3 us (98%)
  local copies, waits for them, and re-layouts  1.54 us (2%)
    pallas_call x1, Pallas kernels, on_device(): pl.pallas_call(kernel, out_shape=jax.ShapeDtypeStruct((ROWS, WIDTH), BF16...  85.3 us

profile of v4, /device:TPU:32, one launch (start us, length us, event | category | flops | bytes accessed | tf_op | source)
XLA Modules:
  0.0 86.8 jit_solution(12993610519251308063)
XLA Ops:
  0.0 85.3 %shard_map.109 = bf16[16,3072]{1,0:T(8,128)(2,1)} custom-call(s32[64]{0:T(128)} %prompt_ids.1, s32[1,4]{1,0:T(1,128)} %lengths.1, bf16[256,256]{1,0:T(8,128)(2,1)} %bitcast.14, bf16[256,3072]{1,0:T(8,128)(2,1)} %ctx_hbm.1, bf16[16,3072]{1,0:T(8,128)(2,1)} %bitcast.15, f32[4,3,2,3072]{3,2,1,0:T(2,128)} %bitcast.12, f32[4,2,2,3072]{3,2,1,0:T(2,128)} %bitcast.13, ...), custom_call_target="tpu_custom_call" | custom-call | tf_op jit(solution)/shard_map/pallas_call | solution.py:635
  85.3 1.5 %copy.13 = bf16[1,16,3072]{2,1,0:T(8,128)(2,1)} copy(bf16[1,16,3072]{2,1,0:T(8,128)(2,1)} %bitcast.11) | data formatting | bytes 196608

commit v5 on v4

--- a/solution.py
+++ b/solution.py
@@ -15,6 +15,7 @@
 DEPTH = 8
 HEAD = 128
 STEPS = (1, -1, 2)
+LINES = (0, -1, 1, 2)
 
 
 def layer_norm(values):
@@ -90,11 +91,15 @@
                     for onward in (2, 1, -1):
                         self.pass_on(half, 0, 2, half, onward, 8)
 
+    def finish_line(self, half, index):
+        if index in (1, 2):
+            await_bytes(self.buf.at[half, self.place.slot(half, 0, LINES[index])], self.sems.at[half, 2 + index])
+        if index > 0:
+            await_bytes(self.buf.at[half, pl.ds(0, 3)], self.sems.at[half, 5 + index])
+
     def finish(self, half):
-        for index in (0, 1):
-            await_bytes(self.buf.at[half, self.place.slot(half, 0, -STEPS[index])], self.sems.at[half, 3 + index])
-        for index in (6, 7, 8):
-            await_bytes(self.buf.at[half, pl.ds(0, 3)], self.sems.at[half, index])
+        for index in range(4):
+            self.finish_line(half, index)
 
     def close(self):
         await_bytes(self.buf.at[:, pl.ds(0, 15)], self.send)
@@ -174,54 +179,40 @@
 
 
 class Handoff:
-    def __init__(self, place, buf, sems, sibling_sems, send):
-        self.place, self.buf, self.sems, self.sibling_sems, self.send = place, buf, sems, sibling_sems, send
+    def __init__(self, place, buf, sems, send):
+        self.place, self.buf, self.sems, self.send = place, buf, sems, send
 
     def slot(self, step):
-        return lax.rem(self.place.z + step + DEPTH, DEPTH) * 2 + self.place.core
+        return lax.rem(self.place.z + step + DEPTH, DEPTH)
 
     def onward(self, piece, side, held, goal):
         way = (1, -1)[side]
         ref = self.buf.at[piece, self.slot(-way * held)]
         push(ref, ref, self.send, self.sems.at[piece, side, goal - 1], self.place.up(way * (goal - held)))
 
-    def across(self, piece, slot):
-        ref = self.buf.at[piece, slot]
-        push(ref, ref, self.send, self.sibling_sems.at[piece], self.place.sibling())
-
     def take(self, piece, side, number):
-        slot = self.slot(-(1, -1)[side] * number)
-        await_bytes(self.buf.at[piece, slot], self.sems.at[piece, side, number - 1])
-        return slot
+        await_bytes(self.buf.at[piece, self.slot(-(1, -1)[side] * number)], self.sems.at[piece, side, number - 1])
 
     def start(self, piece):
         for goal in (2, 1):
             for side in (0, 1):
                 self.onward(piece, side, 0, goal)
-        self.across(piece, self.slot(0))
 
     def pass_on(self, piece):
         for side in (0, 1):
-            slot = self.take(piece, side, 2)
+            self.take(piece, side, 2)
             if piece == side:
                 self.onward(piece, side, 2, 4)
             self.onward(piece, side, 2, 3)
-            self.across(piece, slot)
-
-    def near(self, piece):
-        for side in (0, 1):
-            self.across(piece, self.take(piece, side, 1))
-
-    def far(self, piece):
-        for side in (0, 1):
-            self.across(piece, self.take(piece, side, 3))
-        self.across(piece, self.take(piece, piece, 4))
 
     def finish(self, piece):
-        await_bytes(self.buf.at[piece, pl.ds(0, DEPTH)], self.sibling_sems.at[piece])
+        for number in (1, 3):
+            for side in (0, 1):
+                self.take(piece, side, number)
+        self.take(piece, piece, 4)
 
     def close(self):
-        await_bytes(self.buf.at[:, pl.ds(0, 15)], self.send)
+        await_bytes(self.buf.at[:, pl.ds(0, 7)], self.send)
 
 
 class Update:
@@ -323,8 +314,8 @@
 
 
 def kernel(
-    prompt_ids,
-    lengths,
+    ids_hbm,
+    lengths_hbm,
     prompt_hbm,
     ctx_hbm,
     latent_hbm,
@@ -332,7 +323,7 @@
     tmod_hbm,
     qkv_hbm,
     txt_hbm,
-    gain,
+    gain_hbm,
     proj_hbm,
     out,
     prompt,
@@ -360,8 +351,9 @@
     sc_sends,
     handed,
     hand_sems,
-    hand_siblings,
     hand_send,
+    crossing,
+    cross_sems,
     up_outgoing,
     up_incoming,
     up_products,
@@ -371,8 +363,13 @@
     x_state,
     rows_mod,
     text_in,
-    text_kv,
+    keys_all,
+    values_all,
+    bias,
     tscale,
+    prompt_ids,
+    lengths,
+    gain,
 ):
     place = Place()
 
@@ -393,13 +390,9 @@
     halves = (pl.ds(0, HALF), pl.ds(HALF, HALF))
     load_prompt = load(prompt_hbm, prompt)
     load_ctx = [load(ctx_hbm.at[:, cols], ctx.at[:, cols]) for cols in halves]
+    load_lengths = load(lengths_hbm, lengths)
     load_latent = load(latent_hbm, latent)
     load_imod = load(imod_hbm, imod)
-
-    bounds, running = [], 0
-    for image in range(4):
-        running = running + lengths[0, image]
-        bounds.append(running)
 
     def segments_of(row_ids):
         return sum((row_ids >= bound).astype(jnp.int32) for bound in bounds)
@@ -428,6 +421,8 @@
         place, sc_buf, sc_sides, sc_line, sc_mid, sc_landed, sc_sems, sc_sends, gathered.at[1, :, pl.ds(0, 11)]
     )
     text_scatter.start()
+    load_ids = load(ids_hbm, prompt_ids)
+    load_gain = load(gain_hbm, gain)
     load_proj = [
         load(
             proj_hbm.at[pl.ds(share * 64, 64), pl.ds(half * HALF, HALF)],
@@ -440,6 +435,12 @@
     load_tmod = load(tmod_hbm, tmod)
     load_qkv = [load(qkv_hbm.at[part], qkv_w.at[:, pl.ds(part * HEAD, HEAD)]) for part in range(3)]
 
+    load_lengths.wait()
+    bounds, running = [], 0
+    for image in range(4):
+        running = running + lengths[0, image]
+        bounds.append(running)
+
     load_imod.wait()
     mine = segments_of(place.tp * ROWS + lax.broadcasted_iota(jnp.int32, (ROWS, 1), 0))
     for step in (0, 1):
@@ -467,9 +468,9 @@
     first_gather = gather_of(0)
     first_gather.start()
 
-    handoff = Handoff(place, handed, hand_sems, hand_siblings, hand_send)
+    handoff = Handoff(place, handed, hand_sems, hand_send)
     for half in (0, 1):
-        handed[half, place.group] = text_scatter.result(half).astype(BF16)
+        handed[half, place.z] = text_scatter.result(half).astype(BF16)
         handoff.start(half)
     first_gather.forward()
     for half in (0, 1):
@@ -478,9 +479,6 @@
         copy.wait()
     weights = ProjectionWeights(place, proj_w, proj_sems, proj_sibling, proj_send)
     weights.start()
-
-    for half in (0, 1):
-        handoff.near(half)
 
     load_txt.wait()
     unweave = (col == lax.rem(row, 128) * 2 + row // 128).astype(BF16)
@@ -503,21 +501,34 @@
                 rows = jnp.where(slot_image == image, tmod[image, step, kind : kind + 1, :], rows)
             tscale[step, kind] = rows + float(kind)
 
-    pick_row = lax.broadcasted_iota(jnp.int32, (ROWS, 256), 0)
-    pick_col = lax.broadcasted_iota(jnp.int32, (ROWS, 256), 1)
-    wanted = jnp.zeros((ROWS, 256), jnp.int32)
-    for image in range(4):
-        wanted = jnp.where(pick_row // 4 == image, prompt_ids[place.group * 4 + image] * 4, wanted)
+    segment_rows = segments_of(rows_iota)
+    bias[:, :256] = jnp.where(segment_rows == lax.rem(lanes_iota // 4, 4), 0.0, -1e30)
+    bias[:, 256:] = jnp.where(segment_rows == segments_of(lanes_iota), 0.0, -1e30)
+    values_all[:, HEAD:] = jnp.ones((512, HEAD), BF16)
+
+    pick_row = lax.broadcasted_iota(jnp.int32, (2 * ROWS, HEAD), 0)
+    pick_col = lax.broadcasted_iota(jnp.int32, (2 * ROWS, HEAD), 1)
+    load_ids.wait()
+    wanted = jnp.full((2 * ROWS, HEAD), -1, jnp.int32)
+    for whose, group in enumerate((place.group, place.z * 2 + 1 - place.core)):
+        for image in range(4):
+            prompt_id = prompt_ids[group * 4 + image]
+            held_at = prompt_id // 8 * 16 + lax.rem(prompt_id, 4) * 4
+            held_at = jnp.where(lax.rem(prompt_id // 4, 2) == place.core, held_at, -64)
+            wanted = jnp.where(pick_row // 4 == whose * 4 + image, held_at, wanted)
     pick = (pick_col == wanted + lax.rem(pick_row, 4)).astype(BF16)
-    for half in (0, 1):
-        handoff.far(half)
     taken = []
     for half in (0, 1):
         handoff.finish(half)
         for piece in range(3):
-            held = handed[half, :, :, pl.ds(piece * 512, 512)].reshape(256, 512)
-            taken.append(jnp.dot(pick, held, preferred_element_type=F32))
-    put_block(2, layer_norm(jnp.concatenate(taken, axis=1)).astype(BF16))
+            held = handed[half, :, :, pl.ds(piece * 512, 512)].reshape(HEAD, 512)
+            both = jnp.dot(pick, held, preferred_element_type=F32)
+            taken.append(both[:ROWS])
+            crossing[0, :, pl.ds(half * HALF + piece * 512, 512)] = both[ROWS:].astype(BF16)
+    push(crossing.at[0], crossing.at[1], cross_sems.at[0], cross_sems.at[1], place.sibling())
+    await_bytes(crossing.at[1], cross_sems.at[1])
+    taken = jnp.concatenate(taken, axis=1) + crossing[1].astype(F32)
+    put_block(2, layer_norm(taken).astype(BF16))
     text_gather = gather_of(2)
     text_gather.start()
     weights.relay()
@@ -533,20 +544,16 @@
                 preferred_element_type=F32,
             )
             total = term if total is None else total + term
-        queries = rms_scale(total[:, :HEAD], gain[0:1]).astype(BF16)
-        keys = rms_scale(total[:, HEAD : 2 * HEAD], gain[1:2]).astype(BF16)
-        return queries, keys, total[:, 2 * HEAD :].astype(BF16)
-
-    def project_text(step):
-        for half in (0, 1):
-
-            def modulate(owner, carry):
-                normed = gathered[2, half, owner].astype(F32)
-                scaled = normed * tscale[step, 1, :, halves[half]] + tscale[step, 0, :, halves[half]]
-                text_in[half, owner] = scaled.astype(BF16)
-                return carry
-
-            lax.fori_loop(0, 16, modulate, 0)
+        keys_all[256:, :] = rms_scale(total[:, HEAD : 2 * HEAD], gain[1:2]).astype(BF16)
+        values_all[256:, :HEAD] = total[:, 2 * HEAD :].astype(BF16)
+        return rms_scale(total[:, :HEAD], gain[0:1]).astype(BF16)
+
+    def modulate_text(step, half, slot):
+        normed = gathered[2, half, slot].astype(F32)
+        scaled = normed * tscale[step, 1, :, halves[half]] + tscale[step, 0, :, halves[half]]
+        text_in[half, slot] = scaled.astype(BF16)
+
+    def project_text():
         total = None
         for half in (0, 1):
             term = jnp.dot(
@@ -555,24 +562,14 @@
                 preferred_element_type=F32,
             )
             total = term if total is None else total + term
-        text_kv[:, :HEAD] = rms_scale(total[:, :HEAD], gain[2:3]).astype(BF16)
-        text_kv[:, HEAD:] = total[:, HEAD:].astype(BF16)
-
-    segment_rows = segments_of(rows_iota)
-    text_allowed = segment_rows == lax.rem(lanes_iota // 4, 4)
-    image_allowed = segment_rows == segments_of(lanes_iota)
-
-    def weigh(queries, keys, allowed):
-        scores = lax.dot_general(queries, keys, (((1,), (1,)), ((), ())), preferred_element_type=F32)
-        return jnp.where(allowed, jnp.exp(scores * HEAD**-0.5), 0.0)
-
-    def attend(queries, keys, values):
-        text_part = weigh(queries, text_kv[:, :HEAD], text_allowed)
-        image_part = weigh(queries, keys, image_allowed)
-        norm = jnp.sum(text_part, -1, keepdims=True) + jnp.sum(image_part, -1, keepdims=True)
-        mixed = jnp.dot(text_part.astype(BF16), text_kv[:, HEAD:], preferred_element_type=F32)
-        mixed = mixed + jnp.dot(image_part.astype(BF16), values, preferred_element_type=F32)
-        return (mixed / norm).astype(BF16)
+        keys_all[:256, :] = rms_scale(total[:, :HEAD], gain[2:3]).astype(BF16)
+        values_all[:256, :HEAD] = total[:, HEAD:].astype(BF16)
+
+    def attend(queries):
+        scores = lax.dot_general(queries, keys_all[...], (((1,), (1,)), ((), ())), preferred_element_type=F32)
+        parts = jnp.exp(scores * HEAD**-0.5 + bias[...]).astype(BF16)
+        mixed = jnp.dot(parts, values_all[...], preferred_element_type=F32)
+        return (mixed[:, :HEAD] / mixed[:, HEAD:]).astype(BF16)
 
     def update_of(which):
         parts = (up_outgoing, up_incoming, up_products, up_landed, up_sems, up_sends)
@@ -586,32 +583,48 @@
 
     for copy in load_qkv:
         copy.wait()
-    queries, keys, values = project_image(0, first_gather)
+    load_gain.wait()
+    queries = project_image(0, first_gather)
     weights.last()
-    for half in (0, 1):
-        text_gather.finish(half)
-    project_text(0)
+    for index in range(4):
+        for half in (0, 1):
+            text_gather.finish_line(half, index)
+
+            def modulate_line(first, carry):
+                modulate_text(0, half, place.slot(half, first, LINES[index]))
+                return carry
+
+            lax.fori_loop(0, SIDE, modulate_line, 0)
+    project_text()
 
     first_update = update_of(0)
-    first_update.start(attend(queries, keys, values))
+    first_update.start(attend(queries))
     weights.finish()
     first_update.multiply()
-    project_text(1)
+    for half in (0, 1):
+
+        def modulate_block(slot, carry):
+            modulate_text(1, half, slot)
+            return carry
+
+        lax.fori_loop(0, 16, modulate_block, 0)
+    project_text()
     advance(0, first_update)
 
     put_image(1)
     second_gather = gather_of(1)
     second_gather.start()
     second_gather.forward()
-    queries, keys, values = project_image(1, second_gather)
+    queries = project_image(1, second_gather)
     second_update = update_of(1)
-    second_update.start(attend(queries, keys, values))
+    second_update.start(attend(queries))
     second_update.multiply()
     advance(1, second_update)
     out[...] = x_state[...].astype(BF16)
 
     for part in (text_scatter, first_gather, handoff, weights, text_gather, first_update, second_gather, second_update):
         part.close()
+    await_bytes(crossing.at[0], cross_sems.at[0])
 
 
 def on_device(
@@ -634,8 +647,8 @@
     block = (ROWS, HALF)
     denoised = pl.pallas_call(
         kernel,
-        out_shape=jax.ShapeDtypeStruct((ROWS, WIDTH), BF16),
-        in_specs=[scalars, scalars] + [anywhere] * 7 + [in_vmem, anywhere],
+        out_shape=pltpu.VMEM((ROWS, WIDTH), BF16),
+        in_specs=[anywhere] * 11,
         out_specs=in_vmem,
         scratch_shapes=[
             pltpu.VMEM((256, 256), BF16),
@@ -647,7 +660,7 @@
             pltpu.VMEM((2 * WIDTH, HEAD), BF16),
             pltpu.VMEM((WIDTH, 2 * HEAD), BF16),
             pltpu.VMEM((2, 4, 2, 64, HALF), BF16),
-            dma((14,)),
+            dma((17,)),
             dma((2, 4)),
             dma,
             dma,
@@ -661,10 +674,11 @@
             pltpu.VMEM((2, 6) + block, BF16),
             dma((2, 6)),
             dma((2,)),
-            pltpu.VMEM((2, 16) + block, BF16),
+            pltpu.VMEM((2, 8) + block, BF16),
             dma((2, 2, 4)),
+            dma,
+            pltpu.VMEM((2, ROWS, WIDTH), BF16),
             dma((2,)),
-            dma,
             pltpu.VMEM((2, 2, 4, 4, ROWS, HEAD), BF16),
             pltpu.VMEM((2, 2, 4, 4, ROWS, HEAD), BF16),
             pltpu.VMEM((2, 2, 4) + block, BF16),
@@ -674,8 +688,13 @@
             pltpu.VMEM((ROWS, WIDTH), F32),
             pltpu.VMEM((2, 3, ROWS, WIDTH), F32),
             pltpu.VMEM((2, 16) + block, BF16),
-            pltpu.VMEM((256, 2 * HEAD), BF16),
+            pltpu.VMEM((512, HEAD), BF16),
+            pltpu.VMEM((512, 2 * HEAD), BF16),
+            pltpu.VMEM((256, 512), F32),
             pltpu.VMEM((2, 2, ROWS, WIDTH), F32),
+            pltpu.SMEM((64,), jnp.int32),
+            pltpu.SMEM((1, 4), jnp.int32),
+            pltpu.VMEM((3, HEAD), F32),
         ],
         compiler_params=pltpu.CompilerParams(
             collective_id=0, has_side_effects=True, vmem_limit_bytes=56 * 1024 * 1024

time: 87 us -> 84.3 us (0.969)
  Pallas kernels: 85.3 us -> 83.1 us
  local copies, waits for them, and re-layouts: 1.54 us -> 0.64 us
    pallas_call x1, Pallas kernels: 85.3 us -> 83.1 us  [on_device(): pl.pallas_call(kernel, out_shape=pltpu.VMEM((ROWS, WIDTH), BF16), in_spec...]
    unnamed x1, local copies, waits for them, and re-layouts: 1.54 us -> 0.64 us
where the time goes in v5:
time: 84.3 us; the launch traced here: 83.8 us
  Pallas kernels  83.1 us (99%)
    pallas_call x1, Pallas kernels, on_device(): pl.pallas_call(kernel, out_shape=pltpu.VMEM((ROWS, WIDTH), BF16), in_spec...  83.1 us

profile of v5, /device:TPU:32, one launch (start us, length us, event | category | flops | bytes accessed | tf_op | source)
XLA Modules:
  0.0 83.8 jit_solution(3416267173874437067)
XLA Ops:
  0.0 83.1 %shard_map.109 = bf16[16,3072]{1,0:T(8,128)(2,1)S(1)} custom-call(s32[64]{0:T(128)} %ids_hbm.1, s32[1,4]{1,0:T(1,128)} %lengths_hbm.1, bf16[256,256]{1,0:T(8,128)(2,1)} %bitcast.14, bf16[256,3072]{1,0:T(8,128)(2,1)} %ctx_hbm.1, bf16[16,3072]{1,0:T(8,128)(2,1)} %bitcast.15, f32[4,3,2,3072]{3,2,1,0:T(2,128)} %bitcast.12, f32[4,2,2,3072]{3,2,1,0:T(2,128)} %bitcast.13, ...), custom_call_target="tpu_custom_call" | custom-call | tf_op jit(solution)/shard_map/pallas_call | solution.py:648
  83.1 0.6 copy.13

commit v6 on v5

--- a/solution.py
+++ b/solution.py
@@ -68,10 +68,10 @@
         push(ref, ref, self.send, self.sems.at[half, sem], self.place.along(axis, step))
 
     def start(self):
-        for index in (2, 0, 1):
+        for index in (0, 1, 2):
             for half in (0, 1):
                 self.pass_on(half, 0, 0, half, STEPS[index], index)
-            if index == 2:
+            if index == 1:
                 for half in (0, 1):
                     self.pass_on(half, 0, 0, 1 - half, 2, 5)
         for index in (0, 1):
@@ -193,10 +193,9 @@
     def take(self, piece, side, number):
         await_bytes(self.buf.at[piece, self.slot(-(1, -1)[side] * number)], self.sems.at[piece, side, number - 1])
 
-    def start(self, piece):
-        for goal in (2, 1):
-            for side in (0, 1):
-                self.onward(piece, side, 0, goal)
+    def start(self, piece, goal):
+        for side in (0, 1):
+            self.onward(piece, side, 0, goal)
 
     def pass_on(self, piece):
         for side in (0, 1):
@@ -251,7 +250,7 @@
                 right = self.weights[half, :, :, :, cols].reshape(SIDE * HEAD, 512)
                 product = jnp.dot(left, right, preferred_element_type=F32)
                 self.products[half, :, :, cols] = product.astype(BF16).reshape(SIDE, ROWS, 512)
-            for index, step in enumerate(STEPS):
+            for index, step in ((2, 2), (0, 1), (1, -1)):
                 push(
                     self.products.at[half, lax.rem(first + step + SIDE, SIDE)],
                     self.landed.at[half, index],
@@ -471,7 +470,9 @@
     handoff = Handoff(place, handed, hand_sems, hand_send)
     for half in (0, 1):
         handed[half, place.z] = text_scatter.result(half).astype(BF16)
-        handoff.start(half)
+        handoff.start(half, 2)
+    for half in (0, 1):
+        handoff.start(half, 1)
     first_gather.forward()
     for half in (0, 1):
         handoff.pass_on(half)

time: 84.3 us -> 81.6 us (0.968)
  Pallas kernels: 83.1 us -> 80.8 us
    pallas_call x1, Pallas kernels: 83.1 us -> 80.8 us  [on_device(): pl.pallas_call(kernel, out_shape=pltpu.VMEM((ROWS, WIDTH), BF16), in_spec...]
where the time goes in v6:
time: 81.6 us; the launch traced here: 81.5 us
  Pallas kernels  80.8 us (99%)
    pallas_call x1, Pallas kernels, on_device(): pl.pallas_call(kernel, out_shape=pltpu.VMEM((ROWS, WIDTH), BF16), in_spec...  80.8 us

profile of v6, /device:TPU:32, one launch (start us, length us, event | category | flops | bytes accessed | tf_op | source)
XLA Modules:
  0.0 81.5 jit_solution(16983484768336274839)
XLA Ops:
  0.0 80.8 %shard_map.109 = bf16[16,3072]{1,0:T(8,128)(2,1)S(1)} custom-call(s32[64]{0:T(128)} %ids_hbm.1, s32[1,4]{1,0:T(1,128)} %lengths_hbm.1, bf16[256,256]{1,0:T(8,128)(2,1)} %bitcast.14, bf16[256,3072]{1,0:T(8,128)(2,1)} %ctx_hbm.1, bf16[16,3072]{1,0:T(8,128)(2,1)} %bitcast.15, f32[4,3,2,3072]{3,2,1,0:T(2,128)} %bitcast.12, f32[4,2,2,3072]{3,2,1,0:T(2,128)} %bitcast.13, ...), custom_call_target="tpu_custom_call" | custom-call | tf_op jit(solution)/shard_map/pallas_call | solution.py:649
  80.8 0.6 copy.13

commit v7 on v6

--- a/solution.py
+++ b/solution.py
@@ -224,11 +224,13 @@
 
     def start(self, attended):
         blocks = attended.reshape(SIDE, SIDE, ROWS, HEAD)
-        self.outgoing[0] = blocks
-        for one in range(SIDE):
-            for two in range(SIDE):
-                self.outgoing[1, one, two] = blocks[two, one]
-        for half in (0, 1):
+        for half in (0, 1):
+            if half == 0:
+                self.outgoing[0] = blocks
+            else:
+                for one in range(SIDE):
+                    for two in range(SIDE):
+                        self.outgoing[1, one, two] = blocks[two, one]
             second = self.positions(half)[1]
             for step in (2, 1, -1):
                 push(
@@ -460,7 +462,7 @@
         put_block(step, (values * rows_mod[step, 1] + rows_mod[step, 0]).astype(BF16))
 
     def gather_of(which):
-        return Gather(place, gathered.at[which], gather_sems.at[which], gather_sends.at[which])
+        return Gather(place, gathered.at[which], gather_sems.at[which // 2], gather_sends.at[which])
 
     put_image(0)
     text_scatter.sums()
@@ -579,8 +581,11 @@
     def advance(step, update):
         for half in (0, 1):
             gate = rows_mod[step, 2, :, halves[half]]
-            state = x_state[:, halves[half]] + gate * update.result(half)
-            x_state[:, halves[half]] = state.astype(BF16).astype(F32)
+            state = (x_state[:, halves[half]] + gate * update.result(half)).astype(BF16)
+            if step == 0:
+                x_state[:, halves[half]] = state.astype(F32)
+            else:
+                out[:, halves[half]] = state
 
     for copy in load_qkv:
         copy.wait()
@@ -621,7 +626,6 @@
     second_update.start(attend(queries))
     second_update.multiply()
     advance(1, second_update)
-    out[...] = x_state[...].astype(BF16)
 
     for part in (text_scatter, first_gather, handoff, weights, text_gather, first_update, second_gather, second_update):
         part.close()
@@ -666,7 +670,7 @@
             dma,
             dma,
             pltpu.VMEM((3, 2, 16) + block, BF16),
-            dma((3, 2, 9)),
+            dma((2, 2, 9)),
             dma((3,)),
             pltpu.VMEM((2, 4, 4) + block, BF16),
             pltpu.VMEM((2, 3, 2) + block, BF16),

time: 81.6 us -> 81.4 us (level)
  no operation moved by 1% of the time
where the time goes in v7:
time: 81.4 us; the launch traced here: 81.3 us
  Pallas kernels  80.6 us (99%)
    pallas_call x1, Pallas kernels, on_device(): pl.pallas_call(kernel, out_shape=pltpu.VMEM((ROWS, WIDTH), BF16), in_spec...  80.6 us

profile of v7, /device:TPU:32, one launch (start us, length us, event | category | flops | bytes accessed | tf_op | source)
XLA Modules:
  0.0 81.3 jit_solution(10727597074633447472)
XLA Ops:
  0.0 80.6 %shard_map.109 = bf16[16,3072]{1,0:T(8,128)(2,1)S(1)} custom-call(s32[64]{0:T(128)} %ids_hbm.1, s32[1,4]{1,0:T(1,128)} %lengths_hbm.1, bf16[256,256]{1,0:T(8,128)(2,1)} %bitcast.14, bf16[256,3072]{1,0:T(8,128)(2,1)} %ctx_hbm.1, bf16[16,3072]{1,0:T(8,128)(2,1)} %bitcast.15, f32[4,3,2,3072]{3,2,1,0:T(2,128)} %bitcast.12, f32[4,2,2,3072]{3,2,1,0:T(2,128)} %bitcast.13, ...), custom_call_target="tpu_custom_call" | custom-call | tf_op jit(solution)/shard_map/pallas_call | solution.py:653
  80.7 0.6 copy.13

commit v8 on v7

--- a/solution.py
+++ b/solution.py
@@ -247,11 +247,11 @@
             first = self.positions(half)[0]
             await_bytes(self.incoming.at[half, pl.ds(0, 3)], self.sems.at[half, 0])
             left = jnp.concatenate([self.incoming[half, other].reshape(4 * ROWS, HEAD) for other in range(SIDE)], 1)
-            for piece in range(3):
-                cols = pl.ds(piece * 512, 512)
-                right = self.weights[half, :, :, :, cols].reshape(SIDE * HEAD, 512)
+            for piece in range(2):
+                cols = pl.ds(piece * 768, 768)
+                right = self.weights[half, :, :, :, cols].reshape(SIDE * HEAD, 768)
                 product = jnp.dot(left, right, preferred_element_type=F32)
-                self.products[half, :, :, cols] = product.astype(BF16).reshape(SIDE, ROWS, 512)
+                self.products[half, :, :, cols] = product.astype(BF16).reshape(SIDE, ROWS, 768)
             for index, step in ((2, 2), (0, 1), (1, -1)):
                 push(
                     self.products.at[half, lax.rem(first + step + SIDE, SIDE)],

time: 81.4 us -> 81.4 us (level)
  no operation moved by 1% of the time
where the time goes in v8:
time: 81.4 us; the launch traced here: 81.3 us
  Pallas kernels  80.6 us (99%)
    pallas_call x1, Pallas kernels, on_device(): pl.pallas_call(kernel, out_shape=pltpu.VMEM((ROWS, WIDTH), BF16), in_spec...  80.6 us

profile of v8, /device:TPU:32, one launch (start us, length us, event | category | flops | bytes accessed | tf_op | source)
XLA Modules:
  0.0 81.3 jit_solution(10727597074633447472)
XLA Ops:
  0.0 80.6 %shard_map.109 = bf16[16,3072]{1,0:T(8,128)(2,1)S(1)} custom-call(s32[64]{0:T(128)} %ids_hbm.1, s32[1,4]{1,0:T(1,128)} %lengths_hbm.1, bf16[256,256]{1,0:T(8,128)(2,1)} %bitcast.14, bf16[256,3072]{1,0:T(8,128)(2,1)} %ctx_hbm.1, bf16[16,3072]{1,0:T(8,128)(2,1)} %bitcast.15, f32[4,3,2,3072]{3,2,1,0:T(2,128)} %bitcast.12, f32[4,2,2,3072]{3,2,1,0:T(2,128)} %bitcast.13, ...), custom_call_target="tpu_custom_call" | custom-call | tf_op jit(solution)/shard_map/pallas_call | solution.py:653
  80.7 0.6 copy.13
